TPU v7x, 128 devices: a whole 4x4x4 slice. The times are simulated.
128 devices in a mesh: cells: 16 (over x, z_lo, core), pairs: 8 (over y, z_hi).
Axes of the slice: x: 4, y: 4, z: 4 (z_hi: 2, z_lo: 2; z = z_hi * 2 + z_lo), core: 2. Of those that a mesh axis runs over, the one named last changes fastest.
Arguments:
- number: float32 [64, 128, 4096], P(None, None, 'cells'), may hold values from 0.25 to 2.5
- mix: float32 [3, 4096], P(None, 'cells'), may hold values from 0.05 to 0.3
- neighbours: int32 [3, 4096], P(None, 'cells'), may hold values from 0 to 383, as said below
- sends: int32 [2, 1024], P(None, 'cells'), may hold values from 0 to 255, as said below
- kernel: float32 [128, 128], replicated, may hold values from 0.0005 to 0.005
- growth: float32 [128], replicated, may hold values from 0.05 to 0.5
- brk_rate: float32 [128], replicated, may hold values from 0.02 to 0.3
- brk_target: int32 [2, 128], replicated, may hold values from 0 to 126, as said below
Outputs:
- updated: float32 [64, 128, 4096], P(None, 'pairs', 'cells')
Inputs may be any that keep to these rules, and one draw needn't show every extreme that they name: `sends`: within one partition's block of 64 entries of a row the columns are distinct, each in 0 to 255. `neighbours`: partition 0 never names the lower partition's slots and the last partition never names the upper partition's; every other partition names each of its 128 received slots. `brk_target`: each target of pivot i is below i; both targets of pivot 0 are 0.
All inputs are finite; a program needn't handle non-finite values.
Results may differ from a plain program's by a relative error of at most 0.00005.
Values sent between devices are 32-bit elements; how exact they have to be, the bound alone decides.
No kernel may reach another device: no remote copies, remote signals or barrier semaphores. Data moves between devices by JAX's collectives and lax.ppermute only.
A program may use at most 128 MiB of HBM per device.

v0:
```python
import jax
import jax.numpy as jnp
from jax import lax
from jax.sharding import PartitionSpec as P


def shifted(value, axis, by):
    length = lax.axis_size(axis)
    pairs = [(i, i + by) for i in range(length) if 0 <= i + by < length]
    return lax.ppermute(value, axis, pairs)


def share_of(target, volume, count):
    vk = jnp.exp2(target * 0.25)
    vprev = jnp.exp2((target - 1.0) * 0.25)
    vnext = jnp.exp2((target + 1.0) * 0.25)
    lower = jnp.where(
        (target >= 1.0) & (volume > vprev) & (volume <= vk), (volume - vprev) / (vk - vprev), 0.0
    )
    upper = jnp.where(
        (target <= count - 2.0) & (volume > vk) & (volume < vnext),
        (vnext - volume) / (vnext - vk),
        0.0,
    )
    top = jnp.where((target == count - 1.0) & (volume > vk), volume / vk, 0.0)
    return lower + upper + top


def block_births(acc, moved, sym, targets, i_start, i_width, j_start, j_width):
    levels, piv, cols = moved.shape
    first = i_start + jnp.arange(i_width, dtype=jnp.int32)
    second = j_start + jnp.arange(j_width, dtype=jnp.int32)
    kernel_tile = lax.dynamic_slice(sym, (i_start, j_start), (i_width, j_width))
    mask = jnp.where(
        second[None, :] < first[:, None],
        1.0,
        jnp.where(second[None, :] == first[:, None], 0.5, 0.0),
    ).astype(jnp.float32)
    weight = kernel_tile * mask
    volume = (
        jnp.exp2(first.astype(jnp.float32) * 0.25)[:, None]
        + jnp.exp2(second.astype(jnp.float32) * 0.25)[None, :]
    ).reshape(-1)
    split = share_of(targets, volume[None, :], float(piv))
    split = jnp.where(targets <= piv - 1.0, split, 0.0)
    near_i = lax.dynamic_slice_in_dim(moved, i_start, i_width, 1)
    near_j = lax.dynamic_slice_in_dim(moved, j_start, j_width, 1)
    rate = (weight[None, :, :, None] * near_i[:, :, None, :] * near_j[:, None, :, :]).reshape(
        levels, i_width * j_width, cols
    )
    return acc + jnp.einsum("kp,lpc->lkc", split, rate, precision=lax.Precision.HIGHEST)


def spill_births(moved, sym, own_start, width, count):
    levels, piv, cols = moved.shape
    targets = (own_start + jnp.arange(2 * width, dtype=jnp.int32)).astype(jnp.float32)[:, None]

    def one_block(step, acc):
        return block_births(acc, moved, sym, targets, own_start, width, step * width, width)

    empty = jnp.zeros((levels, 2 * width, cols), jnp.float32)
    return lax.fori_loop(0, count, one_block, empty)


def on_device(number, mix, neighbours, sends, kernel, growth, brk_rate, brk_target):
    levels, piv, cols = number.shape
    n_pairs = lax.axis_size("pairs")
    rank = lax.axis_index("pairs")
    width = piv // n_pairs
    own_start = rank * width
    send_up = sends[0]
    send_down = sends[1]
    from_low = shifted(jnp.take(number, send_up, axis=2), "cells", 1)
    from_high = shifted(jnp.take(number, send_down, axis=2), "cells", -1)
    extended = jnp.concatenate([number, from_low, from_high], axis=2)
    moved = number
    for edge in range(3):
        value = jnp.take(extended, neighbours[edge], axis=2)
        moved = moved + mix[edge][None, None, :] * (value - number)
    sym = 0.5 * (kernel + kernel.T)
    spread = spill_births(moved, sym, own_start, width, rank + 1)
    arrived = shifted(spread[:, width:], "pairs", 1)
    mine = spread[:, :width] + arrived
    own_moved = lax.dynamic_slice_in_dim(moved, own_start, width, 1)
    sym_rows = lax.dynamic_slice_in_dim(sym, own_start, width, 0)
    loss = own_moved * jnp.einsum("ij,ljc->lic", sym_rows, moved, precision=lax.Precision.HIGHEST)
    flux = growth[None, :, None] * moved
    inflow = jnp.concatenate([jnp.zeros_like(flux[:, :1]), flux[:, :-1]], axis=1)
    grow = lax.dynamic_slice_in_dim(inflow - flux, own_start, width, 1)
    index = jnp.arange(piv, dtype=jnp.int32)
    rows = own_start + jnp.arange(width, dtype=jnp.int32)
    counts = (brk_target[0][None, :] == rows[:, None]).astype(jnp.float32) + (
        brk_target[1][None, :] == rows[:, None]
    ).astype(jnp.float32)
    matrix = counts * brk_rate[None, :] - jnp.where(
        rows[:, None] == index[None, :], brk_rate[None, :], 0.0
    )
    gain = jnp.einsum("ki,lic->lkc", matrix, moved, precision=lax.Precision.HIGHEST)
    return own_moved + mine - loss + grow + gain


def solution(mesh):
    placed = (
        P(None, None, "cells"),
        P(None, "cells"),
        P(None, "cells"),
        P(None, "cells"),
        P(),
        P(),
        P(),
        P(),
    )
    return jax.shard_map(
        on_device, mesh=mesh, in_specs=placed, out_specs=P(None, "pairs", "cells"), check_vma=False
    )
```

profile of v0, /device:TPU:120, one launch (start us, length us, event | category | flops | bytes accessed | tf_op | source)
XLA Modules:
  0.0 374.5 jit_solution(3487869705448803522)
XLA Ops:
  0.0 0.8 compare_and_fusion.7
  0.8 8.8 %copy.12 = f32[64,128,256]{1,0,2:T(8,128)} copy(f32[64,128,256]{2,1,0:T(8,128)} %param.14) | data formatting | bytes 16777216 | tf_op args[0]
  9.5 4.1 %gather_fusion = f32[64,64,128]{2,1,0:T(8,128)S(1)} fusion(f32[64,128,256]{1,0,2:T(8,128)} %copy.12, s32[1024]{0:T(1024)S(1)} %pad_clamp_fusion.4), kind=kCustom, calls=%fused_computation.clone | custom fusion | bytes 4194560 | tf_op jit(solution)/shard_map/jit(_take)/gather | solution.py:73
  13.6 1.5 select_bitcast_fusion.1
  15.2 1.9 collective-permute-start
  17.1 4.1 %gather_fusion.1 = f32[64,64,128]{2,1,0:T(8,128)S(1)} fusion(f32[64,128,256]{1,0,2:T(8,128)} %copy.12, s32[1024]{0:T(1024)S(1)} %pad_clamp_fusion.3), kind=kCustom, calls=%fused_computation.2.clone | custom fusion | bytes 4194560 | tf_op jit(solution)/shard_map/jit(_take)/gather | solution.py:74
  21.2 1.5 select_bitcast_fusion
  22.7 3.6 collective-permute-start.1
  26.6 38.7 %collective-permute-done = f32[64,128,64]{1,0,2:T(8,128)} collective-permute-done((f32[64,128,64]{1,0,2:T(8,128)}, f32[64,128,64]{1,0,2:T(8,128)}, u32[]{:S(2)}, u32[]{:S(2)}) %collective-permute-start) | collective-permute-done | bytes 2097184 | tf_op jit(solution)/shard_map/ppermute | solution.py:10
  65.3 10.8 %pad_maximum_fusion = f32[64,128,384]{1,0,2:T(8,128)} fusion(f32[64,128,64]{1,0,2:T(8,128)S(1)} %collective-permute-done.1, f32[64,128,64]{1,0,2:T(8,128)} %collective-permute-done, f32[64,128,256]{1,0,2:T(8,128)} %copy.12), kind=kLoop, calls=%fused_computation.65 | loop fusion | flops 6291456 | bytes 25165824 | tf_op jit(solution)/shard_map/concatenate | solution.py:75
  76.1 8.9 %gather_fusion.3 = f32[256,64,128]{2,1,0:T(8,128)} fusion(f32[64,128,384]{1,0,2:T(8,128)} %pad_maximum_fusion, s32[1024]{0:T(1024)S(1)} %pad_clamp_fusion.1), kind=kCustom, calls=%fused_computation.3.clone | custom fusion | bytes 16778240 | tf_op jit(solution)/shard_map/jit(_take)/gather | solution.py:78
  85.0 9.3 %copy.14 = f32[256,64,128]{0,2,1:T(8,128)} copy(f32[256,64,128]{2,1,0:T(8,128)} %gather_fusion.3) | data formatting | bytes 16777216 | tf_op jit(solution)/shard_map/jit(_take)/gather | solution.py:78
  94.2 9.0 %gather_fusion.4 = f32[256,64,128]{2,1,0:T(8,128)} fusion(f32[64,128,384]{1,0,2:T(8,128)} %pad_maximum_fusion, s32[1024]{0:T(1024)S(1)} %pad_clamp_fusion), kind=kCustom, calls=%fused_computation.4.clone | custom fusion | bytes 16778240 | tf_op jit(solution)/shard_map/jit(_take)/gather | solution.py:78
  103.2 9.2 %copy.15 = f32[256,64,128]{0,2,1:T(8,128)} copy(f32[256,64,128]{2,1,0:T(8,128)} %gather_fusion.4) | data formatting | bytes 16777216 | tf_op jit(solution)/shard_map/jit(_take)/gather | solution.py:78
  112.4 9.0 %gather_fusion.2 = f32[256,64,128]{2,1,0:T(8,128)} fusion(f32[64,128,384]{1,0,2:T(8,128)} %pad_maximum_fusion, s32[1024]{0:T(1024)S(1)} %pad_clamp_fusion.2), kind=kCustom, calls=%fused_computation.1.clone | custom fusion | bytes 16778240 | tf_op jit(solution)/shard_map/jit(_take)/gather | solution.py:78
  121.5 9.3 %copy.13 = f32[256,64,128]{0,2,1:T(8,128)} copy(f32[256,64,128]{2,1,0:T(8,128)} %gather_fusion.2) | data formatting | bytes 16777216 | tf_op jit(solution)/shard_map/jit(_take)/gather | solution.py:78
  130.8 18.8 %broadcast_multiply_fusion = (f32[64,128,256]{2,1,0:T(8,128)}, f32[64,128,256]{2,1,0:T(8,128)}) fusion(f32[128]{0:T(128)S(1)} %copy-done.6, f32[64,128,256]{2,1,0:T(8,128)} %param.14, f32[256,64,128]{0,2,1:T(8,128)} %copy.15, pred[256]{0:T(512)(128)(4,1)S(1)} %get-tuple-element.238, f32[256]{0:T(256)S(1)} %bitcast.130, f32[256,64,128]{0,2,1:T(8,128)} %copy.14, ...), kind=kLoop, calls=%fused_computation.76 | loop fusion | flops 27262976 | bytes 50336000 | tf_op jit(solution)/shard_map/mul | solution.py:87
  149.5 1.3 constant_dynamic-slice_fusion.1
  150.8 0.2 broadcast_in_dim.98
  151.1 197.5 %while.15 = (s32[]{:T(128)}, f32[64,32,256]{2,1,0:T(8,128)S(1)}, s32[]{:T(128)}, f32[128,128]{1,0:T(8,128)S(1)}, s32[]{:T(128)}, /*index=5*/s32[]{:T(128)}, f32[...) while((s32[]{:T(128)}, f32[64,32,256]{2,1,0:T(8,128)S(1)}, ...), condition=%wide.region_1.4_spmd.clone.clone, body=%wide.region_0.3_spmd.clone.clone.sunk | while | flops 1619692032 | bytes 41954512 | solution.py:62
  151.5 1.3 constant_dynamic-slice_fusion.3
  152.8 8.8 %bitcast_multiply_fusion.3 = f32[64,256,256]{2,1,0:T(8,128)} fusion(f32[64,16,256]{2,1,0:T(8,128)S(1)} %constant_dynamic-slice_fusion.3, f32[64,16,256]{2,1,0:T(8,128)S(1)} %get-tuple-element.344, f32[256]{0:T(256)S(1)} %mul.209), kind=kLoop, calls=%fused_computation.6.clone.1 | loop fusion | flops 8388608 | bytes 18875392 | tf_op jit(solution)/shard_map/while/body/mul | solution.py:48
  161.8 14.1 %bitcast_add_fusion.3 = f32[64,32,256]{2,1,0:T(8,128)S(1)} fusion(f32[64,32,256]{2,1,0:T(8,128)S(1)} %get-tuple-element.327, f32[64,256,256]{2,1,0:T(8,128)} %bitcast_multiply_fusion.3, f32[32]{0:T(128)S(1)} %get-tuple-element.304, f32[32]{0:T(128)S(1)} %get-tuple-element.305, f32[256]{0:T(256)S(1)} %add.456, f32[32]{0:T(128)S(1)} %fusion.87, ...), kind=kOutput, calls=%fused_computation.8.clone.1 | convolution fusion | flops 1611300864 | bytes 20973312 | tf_op jit(solution)/shard_map/while/body/kp,lpc->lkc/dot_general | solution.py:51
  176.1 1.3 constant_dynamic-slice_fusion.3
  177.4 8.8 %bitcast_multiply_fusion.3 = f32[64,256,256]{2,1,0:T(8,128)} fusion(f32[64,16,256]{2,1,0:T(8,128)S(1)} %constant_dynamic-slice_fusion.3, f32[64,16,256]{2,1,0:T(8,128)S(1)} %get-tuple-element.344, f32[256]{0:T(256)S(1)} %mul.209), kind=kLoop, calls=%fused_computation.6.clone.1 | loop fusion | flops 8388608 | bytes 18875392 | tf_op jit(solution)/shard_map/while/body/mul | solution.py:48
  186.5 14.1 %bitcast_add_fusion.3 = f32[64,32,256]{2,1,0:T(8,128)S(1)} fusion(f32[64,32,256]{2,1,0:T(8,128)S(1)} %get-tuple-element.327, f32[64,256,256]{2,1,0:T(8,128)} %bitcast_multiply_fusion.3, f32[32]{0:T(128)S(1)} %get-tuple-element.304, f32[32]{0:T(128)S(1)} %get-tuple-element.305, f32[256]{0:T(256)S(1)} %add.456, f32[32]{0:T(128)S(1)} %fusion.87, ...), kind=kOutput, calls=%fused_computation.8.clone.1 | convolution fusion | flops 1611300864 | bytes 20973312 | tf_op jit(solution)/shard_map/while/body/kp,lpc->lkc/dot_general | solution.py:51
  200.8 1.3 constant_dynamic-slice_fusion.3
  202.1 8.8 %bitcast_multiply_fusion.3 = f32[64,256,256]{2,1,0:T(8,128)} fusion(f32[64,16,256]{2,1,0:T(8,128)S(1)} %constant_dynamic-slice_fusion.3, f32[64,16,256]{2,1,0:T(8,128)S(1)} %get-tuple-element.344, f32[256]{0:T(256)S(1)} %mul.209), kind=kLoop, calls=%fused_computation.6.clone.1 | loop fusion | flops 8388608 | bytes 18875392 | tf_op jit(solution)/shard_map/while/body/mul | solution.py:48
  211.1 14.1 %bitcast_add_fusion.3 = f32[64,32,256]{2,1,0:T(8,128)S(1)} fusion(f32[64,32,256]{2,1,0:T(8,128)S(1)} %get-tuple-element.327, f32[64,256,256]{2,1,0:T(8,128)} %bitcast_multiply_fusion.3, f32[32]{0:T(128)S(1)} %get-tuple-element.304, f32[32]{0:T(128)S(1)} %get-tuple-element.305, f32[256]{0:T(256)S(1)} %add.456, f32[32]{0:T(128)S(1)} %fusion.87, ...), kind=kOutput, calls=%fused_computation.8.clone.1 | convolution fusion | flops 1611300864 | bytes 20973312 | tf_op jit(solution)/shard_map/while/body/kp,lpc->lkc/dot_general | solution.py:51
  225.5 1.3 constant_dynamic-slice_fusion.3
  226.8 8.8 %bitcast_multiply_fusion.3 = f32[64,256,256]{2,1,0:T(8,128)} fusion(f32[64,16,256]{2,1,0:T(8,128)S(1)} %constant_dynamic-slice_fusion.3, f32[64,16,256]{2,1,0:T(8,128)S(1)} %get-tuple-element.344, f32[256]{0:T(256)S(1)} %mul.209), kind=kLoop, calls=%fused_computation.6.clone.1 | loop fusion | flops 8388608 | bytes 18875392 | tf_op jit(solution)/shard_map/while/body/mul | solution.py:48
  235.8 14.1 %bitcast_add_fusion.3 = f32[64,32,256]{2,1,0:T(8,128)S(1)} fusion(f32[64,32,256]{2,1,0:T(8,128)S(1)} %get-tuple-element.327, f32[64,256,256]{2,1,0:T(8,128)} %bitcast_multiply_fusion.3, f32[32]{0:T(128)S(1)} %get-tuple-element.304, f32[32]{0:T(128)S(1)} %get-tuple-element.305, f32[256]{0:T(256)S(1)} %add.456, f32[32]{0:T(128)S(1)} %fusion.87, ...), kind=kOutput, calls=%fused_computation.8.clone.1 | convolution fusion | flops 1611300864 | bytes 20973312 | tf_op jit(solution)/shard_map/while/body/kp,lpc->lkc/dot_general | solution.py:51
  250.1 1.3 constant_dynamic-slice_fusion.3
  251.4 8.8 %bitcast_multiply_fusion.3 = f32[64,256,256]{2,1,0:T(8,128)} fusion(f32[64,16,256]{2,1,0:T(8,128)S(1)} %constant_dynamic-slice_fusion.3, f32[64,16,256]{2,1,0:T(8,128)S(1)} %get-tuple-element.344, f32[256]{0:T(256)S(1)} %mul.209), kind=kLoop, calls=%fused_computation.6.clone.1 | loop fusion | flops 8388608 | bytes 18875392 | tf_op jit(solution)/shard_map/while/body/mul | solution.py:48
  260.5 14.1 %bitcast_add_fusion.3 = f32[64,32,256]{2,1,0:T(8,128)S(1)} fusion(f32[64,32,256]{2,1,0:T(8,128)S(1)} %get-tuple-element.327, f32[64,256,256]{2,1,0:T(8,128)} %bitcast_multiply_fusion.3, f32[32]{0:T(128)S(1)} %get-tuple-element.304, f32[32]{0:T(128)S(1)} %get-tuple-element.305, f32[256]{0:T(256)S(1)} %add.456, f32[32]{0:T(128)S(1)} %fusion.87, ...), kind=kOutput, calls=%fused_computation.8.clone.1 | convolution fusion | flops 1611300864 | bytes 20973312 | tf_op jit(solution)/shard_map/while/body/kp,lpc->lkc/dot_general | solution.py:51
  274.8 1.3 constant_dynamic-slice_fusion.3
  276.1 8.8 %bitcast_multiply_fusion.3 = f32[64,256,256]{2,1,0:T(8,128)} fusion(f32[64,16,256]{2,1,0:T(8,128)S(1)} %constant_dynamic-slice_fusion.3, f32[64,16,256]{2,1,0:T(8,128)S(1)} %get-tuple-element.344, f32[256]{0:T(256)S(1)} %mul.209), kind=kLoop, calls=%fused_computation.6.clone.1 | loop fusion | flops 8388608 | bytes 18875392 | tf_op jit(solution)/shard_map/while/body/mul | solution.py:48
  285.1 14.1 %bitcast_add_fusion.3 = f32[64,32,256]{2,1,0:T(8,128)S(1)} fusion(f32[64,32,256]{2,1,0:T(8,128)S(1)} %get-tuple-element.327, f32[64,256,256]{2,1,0:T(8,128)} %bitcast_multiply_fusion.3, f32[32]{0:T(128)S(1)} %get-tuple-element.304, f32[32]{0:T(128)S(1)} %get-tuple-element.305, f32[256]{0:T(256)S(1)} %add.456, f32[32]{0:T(128)S(1)} %fusion.87, ...), kind=kOutput, calls=%fused_computation.8.clone.1 | convolution fusion | flops 1611300864 | bytes 20973312 | tf_op jit(solution)/shard_map/while/body/kp,lpc->lkc/dot_general | solution.py:51
  299.5 1.3 constant_dynamic-slice_fusion.3
  300.8 8.8 %bitcast_multiply_fusion.3 = f32[64,256,256]{2,1,0:T(8,128)} fusion(f32[64,16,256]{2,1,0:T(8,128)S(1)} %constant_dynamic-slice_fusion.3, f32[64,16,256]{2,1,0:T(8,128)S(1)} %get-tuple-element.344, f32[256]{0:T(256)S(1)} %mul.209), kind=kLoop, calls=%fused_computation.6.clone.1 | loop fusion | flops 8388608 | bytes 18875392 | tf_op jit(solution)/shard_map/while/body/mul | solution.py:48
  309.8 14.1 %bitcast_add_fusion.3 = f32[64,32,256]{2,1,0:T(8,128)S(1)} fusion(f32[64,32,256]{2,1,0:T(8,128)S(1)} %get-tuple-element.327, f32[64,256,256]{2,1,0:T(8,128)} %bitcast_multiply_fusion.3, f32[32]{0:T(128)S(1)} %get-tuple-element.304, f32[32]{0:T(128)S(1)} %get-tuple-element.305, f32[256]{0:T(256)S(1)} %add.456, f32[32]{0:T(128)S(1)} %fusion.87, ...), kind=kOutput, calls=%fused_computation.8.clone.1 | convolution fusion | flops 1611300864 | bytes 20973312 | tf_op jit(solution)/shard_map/while/body/kp,lpc->lkc/dot_general | solution.py:51
  324.1 1.3 constant_dynamic-slice_fusion.3
  325.4 8.8 %bitcast_multiply_fusion.3 = f32[64,256,256]{2,1,0:T(8,128)} fusion(f32[64,16,256]{2,1,0:T(8,128)S(1)} %constant_dynamic-slice_fusion.3, f32[64,16,256]{2,1,0:T(8,128)S(1)} %get-tuple-element.344, f32[256]{0:T(256)S(1)} %mul.209), kind=kLoop, calls=%fused_computation.6.clone.1 | loop fusion | flops 8388608 | bytes 18875392 | tf_op jit(solution)/shard_map/while/body/mul | solution.py:48
  334.5 14.1 %bitcast_add_fusion.3 = f32[64,32,256]{2,1,0:T(8,128)S(1)} fusion(f32[64,32,256]{2,1,0:T(8,128)S(1)} %get-tuple-element.327, f32[64,256,256]{2,1,0:T(8,128)} %bitcast_multiply_fusion.3, f32[32]{0:T(128)S(1)} %get-tuple-element.304, f32[32]{0:T(128)S(1)} %get-tuple-element.305, f32[256]{0:T(256)S(1)} %add.456, f32[32]{0:T(128)S(1)} %fusion.87, ...), kind=kOutput, calls=%fused_computation.8.clone.1 | convolution fusion | flops 1611300864 | bytes 20973312 | tf_op jit(solution)/shard_map/while/body/kp,lpc->lkc/dot_general | solution.py:51
  348.7 1.6 collective-permute-start.2
  350.3 7.6 %fusion.48 = f32[64,16,256]{2,1,0:T(8,128)S(1)} fusion(f32[64,128,256]{2,1,0:T(8,128)} %get-tuple-element.350, f32[128,128]{1,0:T(8,128)S(1)} %get-tuple-element.354, s32[]{:T(128)} %select_n.81), kind=kOutput, calls=%fused_computation.81 | convolution fusion | flops 402915328 | bytes 10494976 | tf_op jit(solution)/shard_map/ij,ljc->lic/dot_general | solution.py:86
  357.9 9.2 %collective-permute-done.2 = f32[64,16,256]{2,1,0:T(8,128)S(1)} collective-permute-done((f32[64,16,256]{2,1,0:T(8,128)S(1)}, f32[64,16,256]{2,1,0:T(8,128)S(1)}, u32[]{:S(2)}, u32[]{:S(2)}) %collective-permute-start.2) | collective-permute-done | bytes 1048608 | tf_op jit(solution)/shard_map/ppermute | solution.py:10
  367.2 7.3 %fusion.51 = f32[64,16,256]{2,1,0:T(8,128)} fusion(s32[]{:T(128)} %select_n.81, f32[64,127,256]{2,1,0:T(8,128)} %bitcast.124, f32[64,128,256]{2,1,0:T(8,128)} %get-tuple-element.208, f32[64,16,256]{2,1,0:T(8,128)S(1)} %fusion.48, f32[64,16,256]{2,1,0:T(8,128)S(1)} %collective-permute-done.2, f32[64,32,256]{2,1,0:T(8,128)S(1)} %get-tuple-element.148, ...), kind=kOutput, calls=%fused_computation.84 | convolution fusion | flops 404244480 | bytes 23005188 | tf_op jit(solution)/shard_map/ki,lic->lkc/dot_general | solution.py:98
  (119 shorter events, 3.4 us)
Async XLA Ops:
  13.6 12.8 %copy-start.1 = (f32[128,128]{1,0:T(8,128)S(1)}, f32[128,128]{1,0:T(8,128)}, u32[]{:S(2)}) copy-start(f32[128,128]{1,0:T(8,128)} %param.18) | copy-start | bytes 196612
  13.6 12.8 %copy-start.2 = (s32[3,256]{1,0:T(4,128)S(1)}, s32[3,256]{1,0:T(4,128)}, u32[]{:S(2)}) copy-start(s32[3,256]{1,0:T(4,128)} %param.16) | copy-start | bytes 9220
  13.6 13.0 %copy-start.3 = (f32[3,256]{1,0:T(4,128)S(1)}, f32[3,256]{1,0:T(4,128)}, u32[]{:S(2)}) copy-start(f32[3,256]{1,0:T(4,128)} %param.15) | copy-start | bytes 9220
  15.2 50.1 %collective-permute-start = (f32[64,128,64]{1,0,2:T(8,128)}, f32[64,128,64]{1,0,2:T(8,128)}, u32[]{:S(2)}, u32[]{:S(2)}) collective-permute-start(f32[64,128,64]{1,0,2:T(8,128)} %select_bitcast_fusion.1), channel_id=1, source_target_pairs={{0,8},{8,16},{16,24},{24,32},{32,40},{40,48},{48,56},{56,64},{64,7... | collective-permute-start | bytes 6291464 | tf_op jit(solution)/shard_map/ppermute | solution.py:10
  22.7 42.6 %collective-permute-start.1 = (f32[64,128,64]{1,0,2:T(8,128)}, f32[64,128,64]{1,0,2:T(8,128)S(1)}, u32[]{:S(2)}, u32[]{:S(2)}) collective-permute-start(f32[64,128,64]{1,0,2:T(8,128)} %select_bitcast_fusion), channel_id=1, source_target_pairs={{8,0},{16,8},{24,16},{32,24},{40,32},{48,40},{56,48},{64,56},{72,6... | collective-permute-start | bytes 6291464 | tf_op jit(solution)/shard_map/ppermute | solution.py:10
  121.5 9.3 %copy-start.6 = (f32[128]{0:T(128)S(1)}, f32[128]{0:T(128)}, u32[]{:S(2)}) copy-start(f32[128]{0:T(128)} %param.19) | copy-start | bytes 1540
  151.1 199.2 %copy-start.4 = (s32[2,128]{1,0:T(2,128)S(1)}, s32[2,128]{1,0:T(2,128)}, u32[]{:S(2)}) copy-start(s32[2,128]{1,0:T(2,128)} %param.21) | copy-start | bytes 3076
  348.6 18.6 %copy-start = (f32[64,128,256]{2,1,0:T(8,128)S(1)}, f32[64,128,256]{2,1,0:T(8,128)}, u32[]{:S(2)}) copy-start(f32[64,128,256]{2,1,0:T(8,128)} %get-tuple-element.350) | copy-start | bytes 25165828
  348.6 18.6 %copy-start.5 = (f32[128]{0:T(128)S(1)}, f32[128]{0:T(128)}, u32[]{:S(2)}) copy-start(f32[128]{0:T(128)} %param.20) | copy-start | bytes 1540
  348.7 18.5 %collective-permute-start.2 = (f32[64,16,256]{2,1,0:T(8,128)S(1)}, f32[64,16,256]{2,1,0:T(8,128)S(1)}, u32[]{:S(2)}, u32[]{:S(2)}) collective-permute-start(f32[64,16,256]{2,1,0:T(8,128)S(1)} %slice.48), channel_id=1, source_target_pairs={{0,1},{1,2},{2,3},{3,4},{4,5},{5,6},{6,7},{8,9},{9,10},{10,11},{11... | collective-permute-start | bytes 3145736 | tf_op jit(solution)/shard_map/ppermute | solution.py:10
where the time goes:
time: 376 us; the launch traced here: 374 us
  matrix products  128 us (34%)
  other arithmetic  105 us (28%)
  local copies, waits for them, and re-layouts  85.1 us (23%)
  waiting for transfers between devices  47.9 us (13%)
  starting transfers between devices  7.09 us (2%)
    dot_general x8, matrix products, block_births(): jnp.einsum('kp,lpc->lkc', split, rate, precision=lax.Precision.HIGHEST)  113 us
    mul x8, other arithmetic, block_births(): weight[None, :, :, None] * near_i[:, :, None, :] * near_j[:, None, :, :]  70.3 us
    gather x6, local copies, waits for them, and re-layouts, on_device(): value = jnp.take(extended, neighbours[edge], axis=2)  54.7 us
    ppermute x3, waiting for transfers between devices, shifted(): return lax.ppermute(value, axis, pairs)  47.9 us
    mul x1, other arithmetic, on_device(): flux = growth[None, :, None] * moved  18.8 us
    concatenate x1, other arithmetic, on_device(): extended = jnp.concatenate([number, from_low, from_high], axis=2)  10.8 us
    dynamic_slice x8, local copies, waits for them, and re-layouts, block_births(): near_j = lax.dynamic_slice_in_dim(moved, j_start, j_width, 1)  10.4 us
    unnamed x16, local copies, waits for them, and re-layouts  8.88 us
  transfers between devices with their start and end apart: 3, of which 2 were waited for; matrix products, arithmetic and copies ran while one was open for 4% of the time, Pallas kernels for 0%

commit v1 on v0

v1 whole, which is shorter than its diff:
```python
import functools

import jax
import jax.numpy as jnp
import numpy as np
from jax import lax
from jax.experimental import pallas as pl
from jax.experimental.pallas import tpu as pltpu
from jax.sharding import PartitionSpec as P

PIV = 128
COLS = 256
SLOTS = 64
OWN = 16
WIN = 32
ROWS = WIN + 3 * OWN
STEP = 8
F32 = jnp.float32
BF16 = jnp.bfloat16


def share_tables():
    v = 2.0 ** (np.arange(PIV) / 4.0)
    tables = np.zeros((5, PIV, PIV))
    for m in range(5):
        for k in range(m, PIV):
            i = k - m
            for j in range(i + 1):
                u = 2.0 ** ((i + 4) / 4.0) if i == j else v[i] + v[j]
                if i == j and i + 4 < PIV:
                    u = v[i + 4]
                share = 0.0
                if k >= 1 and v[k - 1] < u <= v[k]:
                    share = (u - v[k - 1]) / (v[k] - v[k - 1])
                elif k <= PIV - 2 and v[k] < u < v[k + 1]:
                    share = (v[k + 1] - u) / (v[k + 1] - v[k])
                elif k == PIV - 1 and u > v[k]:
                    share = u / v[k]
                tables[m, k, j] = share * (0.5 if i == j else 1.0)
    return tables.astype(np.float32)


def split(x):
    hi = x.astype(BF16)
    return hi, (x - hi.astype(F32)).astype(BF16)


def dot(a, b):
    return jnp.dot(a, b, preferred_element_type=F32)


def iota(shape, axis):
    return lax.broadcasted_iota(jnp.int32, shape, axis)


def symmetric(kernel_ref):
    k = kernel_ref[...]
    return 0.5 * (k + k.T)


def fill_functionals(full, kernel_ref, growth_ref, rate_ref, target_ref, table_ref):
    sym = symmetric(kernel_ref)
    full[0] = sym * (table_ref[0] - 1.0)
    full[1] = pltpu.roll(sym, 1, 0) * table_ref[1]
    row, col = iota((PIV, PIV), 0), iota((PIV, PIV), 1)
    rate, growth = rate_ref[...], growth_ref[...]
    counts = (target_ref[0:1, :] == row).astype(F32) + (target_ref[1:2, :] == row).astype(F32)
    full[2] = (
        counts * rate
        + jnp.where(row == col, 1.0 - growth - rate, 0.0)
        + jnp.where(row == col + 1, growth, 0.0)
    )


def functionals(full, rank):
    start = pl.multiple_of(rank * OWN, OWN)
    window = iota((WIN, PIV), 1) == iota((WIN, PIV), 0) + (start - (WIN - OWN))
    rows = jnp.concatenate(
        [window.astype(F32)] + [full[m, pl.ds(start, OWN), :] for m in range(3)], axis=0
    )
    hi, lo = split(rows)
    return jnp.concatenate([hi, hi, lo], axis=1)


def ranks():
    rank = lax.axis_index("pairs")
    part = lax.rem(lax.axis_index("cells"), 4)
    flip = lax.rem(rank, 2) * -2 + 1
    to_up = rank + jnp.where(part == 3, flip, 0)
    to_down = rank + jnp.where(part == 0, flip, 0)
    return rank, to_up, to_down


def halo_kernel(
    number, sends, kernel, growth, rate, target, table, up, down, full, pick, func
):
    @pl.when(pl.program_id(0) == 0)
    def _():
        _, to_up, to_down = ranks()
        fill_functionals(full, kernel, growth, rate, target, table)
        func[0] = functionals(full, to_up)
        func[1] = functionals(full, to_down)
        a, b = sends[0:1, :], sends[1:2, :]
        named = jnp.concatenate([a, a + COLS, b, b + COLS], axis=1)
        pick[...] = (iota((2 * COLS, 4 * SLOTS), 0) == named).astype(BF16)

    pairs = STEP // 2
    both = jnp.concatenate(
        [jnp.concatenate([number[2 * q], number[2 * q + 1]], axis=1) for q in range(pairs)],
        axis=0,
    )
    hi, lo = split(both)
    got_hi = dot(hi, pick[...]).astype(BF16)
    got_lo = dot(lo, pick[...]).astype(BF16)
    for q in range(pairs):
        rows = slice(q * PIV, (q + 1) * PIV)
        for way, out in ((0, up), (1, down)):
            lanes = slice(way * 2 * SLOTS, (way + 1) * 2 * SLOTS)
            h, l = got_hi[rows, lanes], got_lo[rows, lanes]
            out[q] = dot(func[way], jnp.concatenate([h, l, h], axis=0))


def local_kernel(
    number, mix, neighbours, kernel, growth, rate, target, table, base, full, mixing, func
):
    @pl.when(pl.program_id(0) == 0)
    def _():
        rank, _, _ = ranks()
        fill_functionals(full, kernel, growth, rate, target, table)
        func[...] = functionals(full, rank)
        row, col = iota((COLS, COLS), 0), iota((COLS, COLS), 1)
        m = mix[...]
        total = jnp.where(row == col, 1.0 - m[0:1] - m[1:2] - m[2:3], 0.0)
        for e in range(3):
            total = total + jnp.where(neighbours[e : e + 1, :] == row, m[e : e + 1], 0.0)
        mixing[0], mixing[1] = split(total)

    parts = []
    for l in range(STEP):
        h, lo = split(number[l])
        parts.append(dot(func[...], jnp.concatenate([h, lo, h], axis=0)))
    t_hi, t_lo = split(jnp.concatenate(parts, axis=0))
    mixed = dot(t_hi, mixing[0]) + dot(t_lo, mixing[0]) + dot(t_hi, mixing[1])
    base[...] = mixed.reshape(STEP, ROWS, COLS)


def update_kernel(base, low, high, mix, neighbours, kernel, table, out, mixing, band):
    @pl.when(pl.program_id(0) == 0)
    def _():
        rank, _, _ = ranks()
        row = iota((4 * SLOTS, COLS), 0)
        inner = lax.rem(row, 2 * SLOTS)
        for a in range(2):
            slot = COLS + jnp.where(row < 2 * SLOTS, 0, SLOTS) + inner - a * SLOTS
            slot = jnp.where((inner >= a * SLOTS) & (inner < (a + 1) * SLOTS), slot, -1)
            total = jnp.zeros((4 * SLOTS, COLS), F32)
            for e in range(3):
                total = total + jnp.where(
                    neighbours[e : e + 1, :] == slot, mix[e : e + 1, :], 0.0
                )
            hi, lo = split(total)
            mixing[0, :, a * COLS : (a + 1) * COLS] = hi
            mixing[1, :, a * COLS : (a + 1) * COLS] = lo
        sym = symmetric(kernel)
        start = pl.multiple_of(rank * OWN, OWN)
        shift = lax.rem(PIV + (WIN - OWN) - rank * OWN, PIV)
        rows = []
        for m in range(2, 5):
            band[0] = pltpu.roll(sym, m, 0) * table[m]
            rows.append(band[0, pl.ds(start, OWN), :])
        moved = pltpu.roll(jnp.concatenate(rows, axis=0), shift, 1)
        band[1, 0 : 3 * OWN, :] = moved

    pairs = STEP // 2
    both = jnp.concatenate(
        [jnp.concatenate([low[q], high[q]], axis=1) for q in range(pairs)], axis=0
    )
    hi, lo = split(both)
    came = dot(hi, mixing[0]) + dot(lo, mixing[0]) + dot(hi, mixing[1])
    w_hi, w_lo = split(band[1, 0 : 3 * OWN, 0:WIN])
    weights = jnp.concatenate([w_hi, w_hi, w_lo], axis=1)
    for l in range(STEP):
        q, a = l // 2, l % 2
        v = base[l] + came[q * ROWS : (q + 1) * ROWS, a * COLS : (a + 1) * COLS]
        window = v[0:WIN]
        n_hi, n_lo = split(window)
        births = dot(weights, jnp.concatenate([n_hi, n_lo, n_hi], axis=0))
        own = WIN - OWN
        total = v[WIN + 2 * OWN : WIN + 3 * OWN] + window[own:] * v[WIN : WIN + OWN]
        total = total + window[own - 1 : WIN - 1] * v[WIN + OWN : WIN + 2 * OWN]
        for m in range(2, 5):
            total = total + window[own - m : WIN - m] * births[(m - 2) * OWN : (m - 1) * OWN]
        out[l] = total


def whole(shape):
    return pl.BlockSpec(shape, lambda s: (0,) * len(shape))


def on_device(number, mix, neighbours, sends, kernel, growth, brk_rate, brk_target):
    levels = number.shape[0]
    steps = levels // STEP
    growth = growth.reshape(1, PIV)
    rate = brk_rate.reshape(1, PIV)
    table = jnp.asarray(share_tables())
    number_spec = pl.BlockSpec((STEP, PIV, COLS), lambda s: (s, 0, 0))
    half_spec = pl.BlockSpec((STEP // 2, ROWS, 2 * SLOTS), lambda s: (s, 0, 0))
    base_spec = pl.BlockSpec((STEP, ROWS, COLS), lambda s: (s, 0, 0))
    weights = [whole((PIV, PIV)), whole((1, PIV)), whole((1, PIV)), whole((2, PIV)), whole((5, PIV, PIV))]
    half = jax.ShapeDtypeStruct((levels // 2, ROWS, 2 * SLOTS), F32)
    params = pltpu.CompilerParams(vmem_limit_bytes=40 * 2**20)

    up, down = pl.pallas_call(
        halo_kernel,
        grid=(steps,),
        in_specs=[number_spec, whole((2, SLOTS))] + weights,
        out_specs=[half_spec, half_spec],
        out_shape=[half, half],
        scratch_shapes=[
            pltpu.VMEM((3, PIV, PIV), F32),
            pltpu.VMEM((2 * COLS, 4 * SLOTS), BF16),
            pltpu.VMEM((2, ROWS, 3 * PIV), BF16),
        ],
        compiler_params=params,
        cost_estimate=pl.CostEstimate(flops=4 * 10**9, bytes_accessed=12 * 10**6, transcendentals=0),
        name="halo",
    )(number, sends, kernel, growth, rate, brk_target, table)

    n_cells, n_pairs = lax.axis_size("cells"), lax.axis_size("pairs")
    up_pairs, down_pairs = [], []
    for d in range(n_cells):
        for p in range(n_pairs):
            if d + 1 < n_cells:
                up_pairs.append((d * n_pairs + p, (d + 1) * n_pairs + (p ^ (d % 4 == 3))))
            if d > 0:
                down_pairs.append((d * n_pairs + p, (d - 1) * n_pairs + (p ^ (d % 4 == 0))))
    low = lax.ppermute(up, ("cells", "pairs"), up_pairs)
    high = lax.ppermute(down, ("cells", "pairs"), down_pairs)

    base = pl.pallas_call(
        local_kernel,
        grid=(steps,),
        in_specs=[number_spec, whole((3, COLS)), whole((3, COLS))] + weights,
        out_specs=base_spec,
        out_shape=jax.ShapeDtypeStruct((levels, ROWS, COLS), F32),
        scratch_shapes=[
            pltpu.VMEM((3, PIV, PIV), F32),
            pltpu.VMEM((2, COLS, COLS), BF16),
            pltpu.VMEM((ROWS, 3 * PIV), BF16),
        ],
        compiler_params=params,
        cost_estimate=pl.CostEstimate(flops=4 * 10**9, bytes_accessed=14 * 10**6, transcendentals=0),
        name="local",
    )(number, mix, neighbours, kernel, growth, rate, brk_target, table)

    return pl.pallas_call(
        update_kernel,
        grid=(steps,),
        in_specs=[
            base_spec,
            half_spec,
            half_spec,
            whole((3, COLS)),
            whole((3, COLS)),
            whole((PIV, PIV)),
            whole((5, PIV, PIV)),
        ],
        out_specs=pl.BlockSpec((STEP, OWN, COLS), lambda s: (s, 0, 0)),
        out_shape=jax.ShapeDtypeStruct((levels, OWN, COLS), F32),
        scratch_shapes=[
            pltpu.VMEM((2, 4 * SLOTS, 2 * COLS), BF16),
            pltpu.VMEM((2, PIV, PIV), F32),
        ],
        compiler_params=params,
        cost_estimate=pl.CostEstimate(flops=3 * 10**9, bytes_accessed=10 * 10**6, transcendentals=0),
        name="update",
    )(base, low, high, mix, neighbours, kernel, table)


def solution(mesh):
    placed = (
        P(None, None, "cells"),
        P(None, "cells"),
        P(None, "cells"),
        P(None, "cells"),
        P(),
        P(),
        P(),
        P(),
    )
    return jax.shard_map(
        on_device, mesh=mesh, in_specs=placed, out_specs=P(None, "pairs", "cells"), check_vma=False
    )
```

time: 376 us -> 44.5 us (0.12)
  the two profiles are of different devices: /device:TPU:120 before, /device:TPU:51 now
where the time goes in v1:
time: 44.5 us; the launch traced here: 44.2 us
  Pallas kernels  17.5 us (39%)
  waiting for transfers between devices  11.7 us (26%)
  local copies, waits for them, and re-layouts  7.88 us (18%)
  starting transfers between devices  6.96 us (16%)
    unnamed x24, local copies, waits for them, and re-layouts  7.88 us
    ppermute x1, waiting for transfers between devices, on_device(): low = lax.ppermute(up, ('cells', 'pairs'), up_pairs)  6.4 us
    pallas_call x1, Pallas kernels, on_device(): pl.pallas_call(local_kernel, grid=(steps,), in_specs=[number_spec, whole(...  6.14 us
    pallas_call x1, Pallas kernels, on_device(): pl.pallas_call(update_kernel, grid=(steps,), in_specs=[base_spec, half_sp...  5.9 us
    pallas_call x1, Pallas kernels, on_device(): pl.pallas_call(halo_kernel, grid=(steps,), in_specs=[number_spec, whole((...  5.48 us
    ppermute x1, waiting for transfers between devices, on_device(): high = lax.ppermute(down, ('cells', 'pairs'), down_pairs)  5.29 us
    ppermute x1, starting transfers between devices, on_device(): low = lax.ppermute(up, ('cells', 'pairs'), up_pairs)  5.04 us
    ppermute x1, starting transfers between devices, on_device(): high = lax.ppermute(down, ('cells', 'pairs'), down_pairs)  1.92 us
  transfers between devices with their start and end apart: 2, of which 2 were waited for; matrix products, arithmetic and copies ran while one was open for 0% of the time, Pallas kernels for 14%

profile of v1, /device:TPU:51, one launch (start us, length us, event | category | flops | bytes accessed | tf_op | source)
XLA Modules:
  0.0 44.2 jit_solution(16173284762067185001)
XLA Ops:
  0.0 0.0 copy-start
  0.0 3.4 %copy-done = f32[64,128,256]{2,1,0:T(8,128)S(1)} copy-done((f32[64,128,256]{2,1,0:T(8,128)S(1)}, f32[64,128,256]{2,1,0:T(8,128)}, u32[]{:S(2)}) %copy-start) | copy-done | bytes 8388632
  3.4 0.0 copy-start.1
  3.4 0.8 %copy-done.1 = f32[128,128]{1,0:T(8,128)S(1)} copy-done((f32[128,128]{1,0:T(8,128)S(1)}, f32[128,128]{1,0:T(8,128)}, u32[]{:S(2)}) %copy-start.1) | copy-done | bytes 65560
  4.2 0.0 copy-start.5
  4.2 0.7 %copy-done.5 = s32[2,64]{1,0:T(2,128)S(1)} copy-done((s32[2,64]{1,0:T(2,128)S(1)}, s32[2,64]{1,0:T(2,128)}, u32[]{:S(2)}) %copy-start.5) | copy-done | bytes 536
  4.9 0.0 copy-start.6
  4.9 0.7 %copy-done.6 = s32[2,128]{1,0:T(2,128)S(1)} copy-done((s32[2,128]{1,0:T(2,128)S(1)}, s32[2,128]{1,0:T(2,128)}, u32[]{:S(2)}) %copy-start.6) | copy-done | bytes 1048
  5.6 0.0 copy-start.8
  5.6 0.7 %copy-done.8 = f32[128]{0:T(128)S(1)} copy-done((f32[128]{0:T(128)S(1)}, f32[128]{0:T(128)}, u32[]{:S(2)}) %copy-start.8) | copy-done | bytes 536
  6.2 0.0 copy-start.9
  6.2 0.7 %copy-done.9 = f32[128]{0:T(128)S(1)} copy-done((f32[128]{0:T(128)S(1)}, f32[128]{0:T(128)}, u32[]{:S(2)}) %copy-start.9) | copy-done | bytes 536
  6.9 0.0 copy-start.10
  6.9 1.0 %copy-done.10 = f32[5,128,128]{2,1,0:T(8,128)S(1)} copy-done((f32[5,128,128]{2,1,0:T(8,128)S(1)}, f32[5,128,128]{2,1,0:T(8,128)}, u32[]{:S(2)}) %copy-start.10) | copy-done | bytes 327704
  7.9 0.0 copy-start.2
  7.9 0.0 copy-start.3
  7.9 0.0 copy-start.4
  7.9 0.0 copy-start.7
  7.9 0.0 copy-start.11
  7.9 5.5 %halo.1 = (f32[32,80,128]{2,1,0:T(8,128)S(1)}, f32[32,80,128]{2,1,0:T(8,128)S(1)}) custom-call(f32[64,128,256]{2,1,0:T(8,128)S(1)} %copy-done, s32[2,64]{1,0:T(2,128)S(1)} %copy-done.5, f32[128,128]{1,0:T(8,128)S(1)} %copy-done.1, f32[1,128]{1,0:T(1,128)S(1)} %bitcast.2, f32[1,128]{1,0:T(1,128)S(1)} %bitcast.4, s32[2,128]{1,0:T(2,128)S(1)} %copy-done.6, ...), custom_call_target="tpu_custom_call" | custom-call | flops 4000000000 | bytes 12000000 | tf_op jit(solution)/shard_map/halo/pallas_call | solution.py:213
  13.4 5.0 %collective-permute-start = (f32[32,80,128]{2,1,0:T(8,128)S(1)}, f32[32,80,128]{2,1,0:T(8,128)S(1)}, u32[]{:S(2)}, u32[]{:S(2)}) collective-permute-start(f32[32,80,128]{2,1,0:T(8,128)S(1)} %get-tuple-element.7), channel_id=1, source_target_pairs={{0,8},{1,9},{2,10},{3,11},{4,12},{5,13},{6,14},{7,15},{8,16},{9,17... | collective-permute-start | bytes 3932168 | tf_op jit(solution)/shard_map/ppermute | solution.py:237
  18.4 1.9 %collective-permute-start.1 = (f32[32,80,128]{2,1,0:T(8,128)S(1)}, f32[32,80,128]{2,1,0:T(8,128)S(1)}, u32[]{:S(2)}, u32[]{:S(2)}) collective-permute-start(f32[32,80,128]{2,1,0:T(8,128)S(1)} %get-tuple-element.8), channel_id=1, source_target_pairs={{8,0},{9,1},{10,2},{11,3},{12,4},{13,5},{14,6},{15,7},{16,8},{17,9... | collective-permute-start | bytes 3932168 | tf_op jit(solution)/shard_map/ppermute | solution.py:238
  20.4 0.0 copy-done.2
  20.4 0.0 copy-done.3
  20.4 0.0 copy-done.4
  20.4 0.0 copy-done.7
  20.4 0.0 copy-done.11
  20.4 6.1 %local.1.base = f32[64,80,256]{2,1,0:T(8,128)S(1)} custom-call(f32[64,128,256]{2,1,0:T(8,128)S(1)} %copy-done, f32[3,256]{1,0:T(4,128)S(1)} %copy-done.3, s32[3,256]{1,0:T(4,128)S(1)} %copy-done.4, f32[128,128]{1,0:T(8,128)S(1)} %copy-done.2, f32[1,128]{1,0:T(1,128)S(1)} %bitcast.3, f32[1,128]{1,0:T(1,128)S(1)} %bitcast.5, s32[2,128]{1,0:T(2,128)S(1)} %copy-done.7, ...), custom_call_target="tpu_custom_call" | custom-call | flops 4000000000 | bytes 14000000 | tf_op jit(solution)/shard_map/local/pallas_call | solution.py:240
  26.5 6.4 %collective-permute-done.low = f32[32,80,128]{2,1,0:T(8,128)S(1)} collective-permute-done((f32[32,80,128]{2,1,0:T(8,128)S(1)}, f32[32,80,128]{2,1,0:T(8,128)S(1)}, u32[]{:S(2)}, u32[]{:S(2)}) %collective-permute-start) | collective-permute-done | bytes 1310752 | tf_op jit(solution)/shard_map/ppermute | solution.py:237
  33.0 5.3 %collective-permute-done.1.high = f32[32,80,128]{2,1,0:T(8,128)S(1)} collective-permute-done((f32[32,80,128]{2,1,0:T(8,128)S(1)}, f32[32,80,128]{2,1,0:T(8,128)S(1)}, u32[]{:S(2)}, u32[]{:S(2)}) %collective-permute-start.1) | collective-permute-done | bytes 1310752 | tf_op jit(solution)/shard_map/ppermute | solution.py:238
  38.2 5.9 %update.1 = f32[64,16,256]{2,1,0:T(8,128)} custom-call(f32[64,80,256]{2,1,0:T(8,128)S(1)} %local.1.base, f32[32,80,128]{2,1,0:T(8,128)S(1)} %collective-permute-done.low, f32[32,80,128]{2,1,0:T(8,128)S(1)} %collective-permute-done.1.high, f32[3,256]{1,0:T(4,128)S(1)} %copy-done.3, s32[3,256]{1,0:T(4,128)S(1)} %copy-done.4, f32[128,128]{1,0:T(8,128)S(1)} %copy-done.2, ...), custom_call_target="tpu_custom_call" | custom-call | flops 3000000000 | bytes 10000000 | tf_op jit(solution)/shard_map/update/pallas_call | solution.py:256
Async XLA Ops:
  0.0 3.4 %copy-start = (f32[64,128,256]{2,1,0:T(8,128)S(1)}, f32[64,128,256]{2,1,0:T(8,128)}, u32[]{:S(2)}) copy-start(f32[64,128,256]{2,1,0:T(8,128)} %number.3) | copy-start | bytes 25165828
  3.4 0.8 %copy-start.1 = (f32[128,128]{1,0:T(8,128)S(1)}, f32[128,128]{1,0:T(8,128)}, u32[]{:S(2)}) copy-start(f32[128,128]{1,0:T(8,128)} %kernel.5) | copy-start | bytes 196612
  4.2 0.7 %copy-start.5 = (s32[2,64]{1,0:T(2,128)S(1)}, s32[2,64]{1,0:T(2,128)}, u32[]{:S(2)}) copy-start(s32[2,64]{1,0:T(2,128)} %sends.1) | copy-start | bytes 1540
  4.9 0.7 %copy-start.6 = (s32[2,128]{1,0:T(2,128)S(1)}, s32[2,128]{1,0:T(2,128)}, u32[]{:S(2)}) copy-start(s32[2,128]{1,0:T(2,128)} %target.3) | copy-start | bytes 3076
  5.6 0.7 %copy-start.8 = (f32[128]{0:T(128)S(1)}, f32[128]{0:T(128)}, u32[]{:S(2)}) copy-start(f32[128]{0:T(128)} %param.14) | copy-start | bytes 1540
  6.2 0.7 %copy-start.9 = (f32[128]{0:T(128)S(1)}, f32[128]{0:T(128)}, u32[]{:S(2)}) copy-start(f32[128]{0:T(128)} %param.15) | copy-start | bytes 1540
  6.9 1.0 %copy-start.10 = (f32[5,128,128]{2,1,0:T(8,128)S(1)}, f32[5,128,128]{2,1,0:T(8,128)}, u32[]{:S(2)}) copy-start(f32[5,128,128]{2,1,0:T(8,128)} %constant.2.clone.table) | copy-start | bytes 983044
  7.9 12.5 %copy-start.2 = (f32[128,128]{1,0:T(8,128)S(1)}, f32[128,128]{1,0:T(8,128)}, u32[]{:S(2)}) copy-start(f32[128,128]{1,0:T(8,128)} %kernel.5) | copy-start | bytes 196612
  7.9 12.5 %copy-start.3 = (f32[3,256]{1,0:T(4,128)S(1)}, f32[3,256]{1,0:T(4,128)}, u32[]{:S(2)}) copy-start(f32[3,256]{1,0:T(4,128)} %mix.3) | copy-start | bytes 9220
  7.9 12.5 %copy-start.4 = (s32[3,256]{1,0:T(4,128)S(1)}, s32[3,256]{1,0:T(4,128)}, u32[]{:S(2)}) copy-start(s32[3,256]{1,0:T(4,128)} %neighbours.3) | copy-start | bytes 9220
  7.9 12.5 %copy-start.7 = (s32[2,128]{1,0:T(2,128)S(1)}, s32[2,128]{1,0:T(2,128)}, u32[]{:S(2)}) copy-start(s32[2,128]{1,0:T(2,128)} %target.3) | copy-start | bytes 3076
  7.9 12.5 %copy-start.11 = (f32[5,128,128]{2,1,0:T(8,128)S(1)}, f32[5,128,128]{2,1,0:T(8,128)}, u32[]{:S(2)}) copy-start(f32[5,128,128]{2,1,0:T(8,128)} %constant.2.clone.table) | copy-start | bytes 983044
  13.4 19.6 %collective-permute-start = (f32[32,80,128]{2,1,0:T(8,128)S(1)}, f32[32,80,128]{2,1,0:T(8,128)S(1)}, u32[]{:S(2)}, u32[]{:S(2)}) collective-permute-start(f32[32,80,128]{2,1,0:T(8,128)S(1)} %get-tuple-element.7), channel_id=1, source_target_pairs={{0,8},{1,9},{2,10},{3,11},{4,12},{5,13},{6,14},{7,15},{8,16},{9,17... | collective-permute-start | bytes 3932168 | tf_op jit(solution)/shard_map/ppermute | solution.py:237
  18.4 19.8 %collective-permute-start.1 = (f32[32,80,128]{2,1,0:T(8,128)S(1)}, f32[32,80,128]{2,1,0:T(8,128)S(1)}, u32[]{:S(2)}, u32[]{:S(2)}) collective-permute-start(f32[32,80,128]{2,1,0:T(8,128)S(1)} %get-tuple-element.8), channel_id=1, source_target_pairs={{8,0},{9,1},{10,2},{11,3},{12,4},{13,5},{14,6},{15,7},{16,8},{17,9... | collective-permute-start | bytes 3932168 | tf_op jit(solution)/shard_map/ppermute | solution.py:238

commit v2 on v0

v2 whole, which is shorter than its diff:
```python
import functools

import jax
import jax.numpy as jnp
import numpy as np
from jax import lax
from jax.experimental import pallas as pl
from jax.experimental.pallas import tpu as pltpu
from jax.sharding import PartitionSpec as P

PIV = 128
COLS = 256
SLOTS = 64
OWN = 16
WIN = 32
ROWS = WIN + 3 * OWN
STEP = 8
SPLITS = ()
NEAR = 1
LOAD = 8
AHEAD = 3
LIMITS = (54, 46, 32)
F32 = jnp.float32
BF16 = jnp.bfloat16


def share_tables():
    v = 2.0 ** (np.arange(PIV) / 4.0)
    tables = np.zeros((5, PIV, PIV))
    for m in range(5):
        for k in range(m, PIV):
            i = k - m
            for j in range(i + 1):
                u = 2.0 ** ((i + 4) / 4.0) if i == j else v[i] + v[j]
                if i == j and i + 4 < PIV:
                    u = v[i + 4]
                share = 0.0
                if k >= 1 and v[k - 1] < u <= v[k]:
                    share = (u - v[k - 1]) / (v[k] - v[k - 1])
                elif k <= PIV - 2 and v[k] < u < v[k + 1]:
                    share = (v[k + 1] - u) / (v[k + 1] - v[k])
                elif k == PIV - 1 and u > v[k]:
                    share = u / v[k]
                tables[m, k, j] = share * (0.5 if i == j else 1.0)
    return tables.astype(np.float32)


def split(x):
    hi = x.astype(BF16)
    return hi, (x - hi.astype(F32)).astype(BF16)


def dot(a, b):
    return jnp.dot(a, b, preferred_element_type=F32)


def iota(shape, axis):
    return lax.broadcasted_iota(jnp.int32, shape, axis)


def symmetric(kernel_ref):
    k = kernel_ref[...]
    return 0.5 * (k + k.T)


def fill_functionals(full, kernel_ref, growth_ref, rate_ref, target_ref, table_ref):
    sym = symmetric(kernel_ref)
    full[0] = sym * (table_ref[0] - 1.0)
    full[1] = pltpu.roll(sym, 1, 0) * table_ref[1]
    row, col = iota((PIV, PIV), 0), iota((PIV, PIV), 1)
    rate, growth = rate_ref[...], growth_ref[...]
    counts = (target_ref[0:1, :] == row).astype(F32) + (target_ref[1:2, :] == row).astype(F32)
    full[2] = (
        counts * rate
        + jnp.where(row == col, 1.0 - growth - rate, 0.0)
        + jnp.where(row == col + 1, growth, 0.0)
    )


def functionals(full, rank):
    start = pl.multiple_of(rank * OWN, OWN)
    window = iota((WIN, PIV), 1) == iota((WIN, PIV), 0) + (start - (WIN - OWN))
    hi, lo = split(jnp.concatenate([full[m, pl.ds(start, OWN), :] for m in range(3)], axis=0))
    top = jnp.concatenate([window.astype(BF16), hi], axis=0)
    return jnp.concatenate(
        [
            jnp.concatenate([top, top], axis=1),
            jnp.concatenate([lo, jnp.zeros_like(lo)], axis=1),
        ],
        axis=0,
    )


def apply(func, hi, lo):
    got = dot(func, jnp.concatenate([hi, lo], axis=0))
    return jnp.concatenate([got[0:WIN], got[WIN:ROWS] + got[ROWS:]], axis=0)


def place():
    rank, cell = lax.axis_index("pairs"), lax.axis_index("cells")
    part, odd = lax.rem(cell, 4), lax.rem(cell, 2)
    partner = rank + jnp.where((part == 0) | (part == 3), 1 - 2 * lax.rem(rank, 2), 0)
    return rank, partner, odd


def pick_two(sent):
    named = jnp.concatenate([sent, sent + COLS], axis=1)
    return (iota((2 * COLS, 2 * SLOTS), 0) == named).astype(BF16)


def start_loads(number, held, sem, cuts):
    loads = [
        pltpu.make_async_copy(
            number.at[pl.ds(a, b - a)], held.at[pl.ds(a - cuts[0], b - a)], sem.at[i]
        )
        for i, (a, b) in enumerate(zip(cuts, cuts[1:]))
    ]
    loads[0].start()
    return loads


def copy_all(sources, targets, sem):
    copies = [
        pltpu.make_async_copy(a, b, sem.at[i]) for i, (a, b) in enumerate(zip(sources, targets))
    ]
    for copy in copies:
        copy.start()
    return copies


def halo_kernel(number, *refs, cuts):
    source, (out, held), small = refs[:6], refs[6:8], refs[8:14]
    full, pick, func, load_sem, small_sem = refs[14:]
    sends, kernel, growth, rate, target, table = small
    loads = start_loads(number, held, load_sem, cuts)
    copies = copy_all((*source[:5], source[5].at[0:2]), small, small_sem)
    for copy in loads[1:AHEAD]:
        copy.start()
    for copy in copies:
        copy.wait()

    _, partner, odd = place()
    fill_functionals(full, kernel, growth, rate, target, table)
    func[...] = functionals(full, partner)
    pick[...] = pick_two(jnp.where(odd == 1, sends[0:1, :], sends[1:2, :]))

    for i, (start, stop) in enumerate(zip(cuts, cuts[1:])):
        loads[i].wait()
        if i + AHEAD < len(loads):
            loads[i + AHEAD].start()
        for s in range(start - cuts[0], stop - cuts[0], STEP):
            both = jnp.concatenate(
                [
                    jnp.concatenate([held[s + 2 * q], held[s + 2 * q + 1]], axis=1)
                    for q in range(STEP // 2)
                ],
                axis=0,
            )
            hi, lo = split(both)
            got_hi = dot(hi, pick[...]).astype(BF16)
            got_lo = dot(lo, pick[...]).astype(BF16)
            for q in range(0, STEP // 2, 2):
                a, b = slice(q * PIV, (q + 1) * PIV), slice((q + 1) * PIV, (q + 2) * PIV)
                got = apply(
                    func[...],
                    jnp.concatenate([got_hi[a], got_hi[b]], axis=1),
                    jnp.concatenate([got_lo[a], got_lo[b]], axis=1),
                )
                out[s // 2 + q] = got[:, 0 : 2 * SLOTS]
                out[s // 2 + q + 1] = got[:, 2 * SLOTS :]


def local_kernel(number, *refs, cuts):
    source, (base, *near), refs = refs[:8], refs[8 : 9 + NEAR], refs[9 + NEAR :]
    came, band, held, small = *refs[:3], refs[3:11]
    full, mixing, func, pick, load_sem, small_sem = refs[11:]
    sends, mix, neighbours, kernel, growth, rate, target, table = small
    loads = start_loads(number, held, load_sem, cuts)
    copies = copy_all(source, small, small_sem)
    for copy in loads[1:AHEAD]:
        copy.start()
    for copy in copies:
        copy.wait()

    rank, _, odd = place()
    fill_functionals(full, kernel, growth, rate, target, table)
    func[...] = functionals(full, rank)
    pick[...] = pick_two(jnp.where(odd == 1, sends[1:2, :], sends[0:1, :]))
    row, col = iota((COLS, COLS), 0), iota((COLS, COLS), 1)
    m = mix[...]
    total = jnp.where(row == col, 1.0 - m[0:1] - m[1:2] - m[2:3], 0.0)
    for e in range(3):
        total = total + jnp.where(neighbours[e : e + 1, :] == row, m[e : e + 1], 0.0)
    mixing[0], mixing[1] = split(total)

    row = iota((4 * SLOTS, COLS), 0)
    inner = lax.rem(row, 2 * SLOTS)
    upper = jnp.where(row < 2 * SLOTS, 1 - odd, odd)
    for a in range(2):
        slot = COLS + upper * SLOTS + inner - a * SLOTS
        slot = jnp.where((inner >= a * SLOTS) & (inner < (a + 1) * SLOTS), slot, -1)
        total = jnp.zeros((4 * SLOTS, COLS), F32)
        for e in range(3):
            total = total + jnp.where(neighbours[e : e + 1, :] == slot, m[e : e + 1], 0.0)
        hi, lo = split(total)
        came[0, :, a * COLS : (a + 1) * COLS] = hi
        came[1, :, a * COLS : (a + 1) * COLS] = lo
    sym = symmetric(kernel)
    start = pl.multiple_of(rank * OWN, OWN)
    shift = lax.rem(PIV + (WIN - OWN) - rank * OWN, PIV)
    rows = []
    for m in range(2, 5):
        full[m - 2] = pltpu.roll(sym, m, 0) * table[m]
        rows.append(full[m - 2, pl.ds(start, OWN), :])
    hi, lo = split(pltpu.roll(jnp.concatenate(rows, axis=0), shift, 1)[:, 0:WIN])
    band[...] = jnp.concatenate([hi, hi, lo], axis=1)

    pairs = STEP // 2
    for i, (start, stop) in enumerate(zip(cuts, cuts[1:])):
        loads[i].wait()
        if i + AHEAD < len(loads):
            loads[i + AHEAD].start()
        for s in range(start, stop, STEP):
            parts = [apply(func[...], *split(held[l])) for l in range(s, s + STEP)]
            t_hi, t_lo = split(jnp.concatenate(parts, axis=0))
            mixed = dot(t_hi, mixing[0]) + dot(t_lo, mixing[0]) + dot(t_hi, mixing[1])
            base[s : s + STEP] = mixed.reshape(STEP, ROWS, COLS)

            def two(t):
                rows = [t[l * ROWS : (l + 1) * ROWS] for l in range(STEP)]
                return jnp.concatenate(
                    [jnp.concatenate(rows[2 * q : 2 * q + 2], axis=1) for q in range(pairs)], axis=0
                )

            got = dot(two(t_hi), pick[...]) + dot(two(t_lo), pick[...])
            piece = near[0].shape[0]
            at = s // 2 % piece
            near[s // 2 // piece][at : at + pairs] = got.reshape(pairs, ROWS, 2 * SLOTS)


def update_kernel(base, came, band, far, *rest, first):
    near = rest[:NEAR]
    piece = near[0].shape[0]
    out, done, store_sem = rest[-3:]
    pairs = STEP // 2
    own = WIN - OWN
    stores = []
    for i, s in enumerate(range(0, done.shape[0], STEP)):
        both = jnp.concatenate(
            [
                jnp.concatenate(
                    [near[(first + s) // 2 // piece][(first + s) // 2 % piece + q], far[s // 2 + q]],
                    axis=1,
                )
                for q in range(pairs)
            ],
            axis=0,
        )
        hi, lo = split(both)
        got = dot(hi, came[0]) + dot(lo, came[0]) + dot(hi, came[1])
        for l in range(STEP):
            q, a = l // 2, l % 2
            v = base[first + s + l] + got[q * ROWS : (q + 1) * ROWS, a * COLS : (a + 1) * COLS]
            window = v[0:WIN]
            n_hi, n_lo = split(window)
            births = dot(band[...], jnp.concatenate([n_hi, n_lo, n_hi], axis=0))
            total = v[WIN + 2 * OWN : WIN + 3 * OWN] + window[own:] * v[WIN : WIN + OWN]
            total = total + window[own - 1 : WIN - 1] * v[WIN + OWN : WIN + 2 * OWN]
            for m in range(2, 5):
                total = total + window[own - m : WIN - m] * births[(m - 2) * OWN : (m - 1) * OWN]
            done[s + l] = total
        stores.append(
            pltpu.make_async_copy(
                done.at[pl.ds(s, STEP)], out.at[pl.ds(first + s, STEP)], store_sem.at[i]
            )
        )
        stores[-1].start()
    for copy in stores:
        copy.wait()


def on_device(number, mix, neighbours, sends, kernel, growth, brk_rate, brk_target):
    levels = number.shape[0]
    growth = growth.reshape(1, PIV)
    rate = brk_rate.reshape(1, PIV)
    table = jnp.asarray(share_tables())
    hbm = pl.BlockSpec(memory_space=pltpu.HBM)
    vmem = pl.BlockSpec(memory_space=pltpu.VMEM)
    shape = jax.ShapeDtypeStruct
    cost = pl.CostEstimate(flops=10**6, bytes_accessed=10**6, transcendentals=0)

    def params(mib):
        return pltpu.CompilerParams(vmem_limit_bytes=mib * 2**20)

    n_cells, n_pairs = lax.axis_size("cells"), lax.axis_size("pairs")
    far_pairs, near_pairs = [], []
    for d in range(n_cells):
        for p in range(n_pairs):
            near_pairs.append((d * n_pairs + p, (d ^ 1) * n_pairs + p))
            to = d + 1 if d % 2 else d - 1
            if 0 <= to < n_cells:
                far_pairs.append((d * n_pairs + p, to * n_pairs + (p ^ (d % 4 in (0, 3)))))

    small = (sends, mix, neighbours, kernel, growth, rate, brk_target, table)
    halo_small = (sends, kernel, growth, rate, brk_target, table)

    def scratch(arrays):
        return [pltpu.VMEM(x.shape, x.dtype) for x in arrays]

    far = []
    for first, last in zip((0,) + SPLITS, SPLITS + (levels,)):
        cuts = tuple(range(first, last + 1, LOAD))
        message = pl.pallas_call(
            functools.partial(halo_kernel, cuts=cuts),
            in_specs=[hbm] * 7,
            out_specs=vmem,
            out_shape=shape(((last - first) // 2, ROWS, 2 * SLOTS), F32),
            scratch_shapes=[pltpu.VMEM((last - first, PIV, COLS), F32)]
            + scratch(halo_small[:5] + (table[0:2],))
            + [
                pltpu.VMEM((3, PIV, PIV), F32),
                pltpu.VMEM((2 * COLS, 2 * SLOTS), BF16),
                pltpu.VMEM((ROWS + 3 * OWN, 2 * PIV), BF16),
                pltpu.SemaphoreType.DMA((len(cuts) - 1,)),
                pltpu.SemaphoreType.DMA((6,)),
            ],
            compiler_params=params(LIMITS[0]),
            cost_estimate=cost,
            name=f"halo{first}",
        )(number, *halo_small)
        far.append((first, lax.ppermute(message, ("cells", "pairs"), far_pairs)))

    cuts = tuple(range(0, levels + 1, LOAD))
    base, *near, came, band = pl.pallas_call(
        functools.partial(local_kernel, cuts=cuts),
        in_specs=[hbm] * 9,
        out_specs=[vmem] * (3 + NEAR),
        out_shape=[shape((levels, ROWS, COLS), F32)]
        + [shape((levels // 2 // NEAR, ROWS, 2 * SLOTS), F32)] * NEAR
        + [shape((2, 4 * SLOTS, 2 * COLS), BF16), shape((3 * OWN, 3 * WIN), BF16)],
        scratch_shapes=[pltpu.VMEM(number.shape, F32)]
        + scratch(small)
        + [
            pltpu.VMEM((3, PIV, PIV), F32),
            pltpu.VMEM((2, COLS, COLS), BF16),
            pltpu.VMEM((ROWS + 3 * OWN, 2 * PIV), BF16),
            pltpu.VMEM((2 * COLS, 2 * SLOTS), BF16),
            pltpu.SemaphoreType.DMA((len(cuts) - 1,)),
            pltpu.SemaphoreType.DMA((len(small),)),
        ],
        compiler_params=params(LIMITS[1]),
        cost_estimate=cost,
        name="local",
    )(number, *small)
    near = [lax.ppermute(x, ("cells", "pairs"), near_pairs) for x in near]

    out = ()
    for first, message in far:
        count = 2 * message.shape[0]
        out = (
            pl.pallas_call(
                functools.partial(update_kernel, first=first),
                in_specs=[vmem] * (4 + NEAR) + [hbm] * len(out),
                out_specs=hbm,
                out_shape=shape((levels, OWN, COLS), F32),
                input_output_aliases={4 + NEAR: 0} if out else {},
                scratch_shapes=[
                    pltpu.VMEM((count, OWN, COLS), F32),
                    pltpu.SemaphoreType.DMA((count // STEP,)),
                ],
                compiler_params=params(LIMITS[2]),
                cost_estimate=cost,
                name=f"update{first}",
            )(base, came, band, message, *near, *out),
        )
    return out[0]


def solution(mesh):
    placed = (
        P(None, None, "cells"),
        P(None, "cells"),
        P(None, "cells"),
        P(None, "cells"),
        P(),
        P(),
        P(),
        P(),
    )
    return jax.shard_map(
        on_device, mesh=mesh, in_specs=placed, out_specs=P(None, "pairs", "cells"), check_vma=False
    )
```

time: 376 us -> 34.2 us (0.09)
  the two profiles are of different devices: /device:TPU:120 before, /device:TPU:101 now
where the time goes in v2:
time: 34.2 us; the launch traced here: 34.1 us
  Pallas kernels  20.9 us (61%)
  waiting for transfers between devices  9.99 us (29%)
  starting transfers between devices  2.86 us (8%)
    ppermute x1, waiting for transfers between devices, on_device(): far.append((first, lax.ppermute(message, ('cells', 'pairs'), far_pairs)))  9.98 us
    pallas_call x1, Pallas kernels, on_device(): pl.pallas_call(functools.partial(local_kernel, cuts=cuts), in_specs=[hbm]...  8.31 us
    pallas_call x1, Pallas kernels, on_device(): pl.pallas_call(functools.partial(halo_kernel, cuts=cuts), in_specs=[hbm]...  8.03 us
    pallas_call x1, Pallas kernels, on_device(): pl.pallas_call(functools.partial(update_kernel, first=first), in_specs=[v...  4.56 us
    ppermute x1, starting transfers between devices, on_device(): far.append((first, lax.ppermute(message, ('cells', 'pairs'), far_pairs)))  2.02 us
    ppermute x1, starting transfers between devices, on_device(): near = [lax.ppermute(x, ('cells', 'pairs'), near_pairs) for x in near]  0.84 us
  transfers between devices with their start and end apart: 2, of which 1 were waited for; matrix products, arithmetic and copies ran while one was open for 0% of the time, Pallas kernels for 24%

profile of v2, /device:TPU:101, one launch (start us, length us, event | category | flops | bytes accessed | tf_op | source)
XLA Modules:
  0.0 34.1 jit_solution(2294124622134747888)
XLA Ops:
  0.0 0.0 copy-start
  0.0 0.0 copy-start.1
  0.0 0.0 copy-start.2
  0.0 0.0 copy-start.3
  0.0 0.0 copy-start.4
  0.0 0.0 copy-start.5
  0.0 0.0 copy-start.6
  0.0 0.0 copy-start.7
  0.1 8.0 %halo0.1 = f32[32,80,128]{2,1,0:T(8,128)} custom-call(f32[64,128,256]{2,1,0:T(8,128)} %number.3, s32[2,64]{1,0:T(2,128)} %refs_0_.3, f32[128,128]{1,0:T(8,128)} %refs_1_.3, f32[1,128]{1,0:T(1,128)} %bitcast.2, f32[1,128]{1,0:T(1,128)} %bitcast.4, s32[2,128]{1,0:T(2,128)} %refs_4_.1, f32[5,128,128]{2,1,0:T(8,128)} %constant.2.clone.refs_7_.refs_5_), custom_call_target="tpu_custom_call" | custom-call | flops 1000000 | bytes 1000000 | tf_op jit(solution)/shard_map/halo0/pallas_call | solution.py:313
  8.1 2.0 %collective-permute-start = (f32[32,80,128]{2,1,0:T(8,128)}, f32[32,80,128]{2,1,0:T(8,128)S(1)}, u32[]{:S(2)}, u32[]{:S(2)}) collective-permute-start(f32[32,80,128]{2,1,0:T(8,128)} %halo0.1), channel_id=1, source_target_pairs={{8,16},{9,17},{10,18},{11,19},{12,20},{13,21},{14,22},{15,23},{16,... | collective-permute-start | bytes 3932168 | tf_op jit(solution)/shard_map/ppermute | solution.py:331
  10.1 0.0 copy-done
  10.1 0.0 copy-done.1
  10.1 0.0 copy-done.2
  10.2 0.0 copy-done.3
  10.2 0.0 copy-done.4
  10.2 0.0 copy-done.5
  10.2 0.0 copy-done.6
  10.2 0.0 copy-done.7
  10.2 8.3 %local.1 = (f32[64,80,256]{2,1,0:T(8,128)S(1)}, f32[32,80,128]{2,1,0:T(8,128)S(1)}, bf16[2,256,512]{2,1,0:T(8,128)(2,1)S(1)}, bf16[48,96]{1,0:T(8,128)(2,1)S(1)}) custom-call(f32[64,128,256]{2,1,0:T(8,128)} %number.3, s32[2,64]{1,0:T(2,128)S(1)} %copy-done.4, f32[3,256]{1,0:T(4,128)S(1)} %copy-done.2, s32[3,256]{1,0:T(4,128)S(1)} %copy-done.3, ...), custom_call_target="tpu_custom_call" | custom-call | flops 1000000 | bytes 1000000 | tf_op jit(solution)/shard_map/local/pallas_call | solution.py:334
  18.5 0.8 %collective-permute-start.1 = (f32[32,80,128]{2,1,0:T(8,128)S(1)}, f32[32,80,128]{2,1,0:T(8,128)S(1)}, u32[]{:S(2)}, u32[]{:S(2)}) collective-permute-start(f32[32,80,128]{2,1,0:T(8,128)S(1)} %get-tuple-element.12), channel_id=1, source_target_pairs={{0,8},{1,9},{2,10},{3,11},{4,12},{5,13},{6,14},{7,15},{8,0},{9,1},... | collective-permute-start | bytes 3932168 | tf_op jit(solution)/shard_map/ppermute | solution.py:355
  19.4 10.0 %collective-permute-done.far = f32[32,80,128]{2,1,0:T(8,128)S(1)} collective-permute-done((f32[32,80,128]{2,1,0:T(8,128)}, f32[32,80,128]{2,1,0:T(8,128)S(1)}, u32[]{:S(2)}, u32[]{:S(2)}) %collective-permute-start) | collective-permute-done | bytes 1310752 | tf_op jit(solution)/shard_map/ppermute | solution.py:331
  29.3 0.0 collective-permute-done.1.rest_0_
  29.4 4.6 %update0.1 = f32[64,16,256]{2,1,0:T(8,128)} custom-call(f32[64,80,256]{2,1,0:T(8,128)S(1)} %get-tuple-element.9.base, bf16[2,256,512]{2,1,0:T(8,128)(2,1)S(1)} %get-tuple-element.10.came, bf16[48,96]{1,0:T(8,128)(2,1)S(1)} %get-tuple-element.11.band, f32[32,80,128]{2,1,0:T(8,128)S(1)} %collective-permute-done.far, ...), custom_call_target="tpu_custom_call" | custom-call | flops 1000000 | bytes 1000000 | tf_op jit(solution)/shard_map/update0/pallas_call | solution.py:361
Async XLA Ops:
  0.0 10.1 %copy-start = (f32[5,128,128]{2,1,0:T(8,128)S(1)}, f32[5,128,128]{2,1,0:T(8,128)}, u32[]{:S(2)}) copy-start(f32[5,128,128]{2,1,0:T(8,128)} %constant.2.clone.refs_7_.refs_5_) | copy-start | bytes 983044
  0.0 10.1 %copy-start.1 = (f32[128,128]{1,0:T(8,128)S(1)}, f32[128,128]{1,0:T(8,128)}, u32[]{:S(2)}) copy-start(f32[128,128]{1,0:T(8,128)} %refs_1_.3) | copy-start | bytes 196612
  0.0 10.1 %copy-start.2 = (f32[3,256]{1,0:T(4,128)S(1)}, f32[3,256]{1,0:T(4,128)}, u32[]{:S(2)}) copy-start(f32[3,256]{1,0:T(4,128)} %refs_1_.2) | copy-start | bytes 9220
  0.0 10.2 %copy-start.3 = (s32[3,256]{1,0:T(4,128)S(1)}, s32[3,256]{1,0:T(4,128)}, u32[]{:S(2)}) copy-start(s32[3,256]{1,0:T(4,128)} %refs_2_.1) | copy-start | bytes 9220
  0.0 10.2 %copy-start.4 = (s32[2,64]{1,0:T(2,128)S(1)}, s32[2,64]{1,0:T(2,128)}, u32[]{:S(2)}) copy-start(s32[2,64]{1,0:T(2,128)} %refs_0_.3) | copy-start | bytes 1540
  0.0 10.2 %copy-start.5 = (s32[2,128]{1,0:T(2,128)S(1)}, s32[2,128]{1,0:T(2,128)}, u32[]{:S(2)}) copy-start(s32[2,128]{1,0:T(2,128)} %refs_4_.1) | copy-start | bytes 3076
  0.0 10.2 %copy-start.6 = (f32[128]{0:T(128)S(1)}, f32[128]{0:T(128)}, u32[]{:S(2)}) copy-start(f32[128]{0:T(128)} %param.14) | copy-start | bytes 1540
  0.0 10.2 %copy-start.7 = (f32[128]{0:T(128)S(1)}, f32[128]{0:T(128)}, u32[]{:S(2)}) copy-start(f32[128]{0:T(128)} %param.15) | copy-start | bytes 1540
  8.1 21.2 %collective-permute-start = (f32[32,80,128]{2,1,0:T(8,128)}, f32[32,80,128]{2,1,0:T(8,128)S(1)}, u32[]{:S(2)}, u32[]{:S(2)}) collective-permute-start(f32[32,80,128]{2,1,0:T(8,128)} %halo0.1), channel_id=1, source_target_pairs={{8,16},{9,17},{10,18},{11,19},{12,20},{13,21},{14,22},{15,23},{16,... | collective-permute-start | bytes 3932168 | tf_op jit(solution)/shard_map/ppermute | solution.py:331
  18.5 10.8 %collective-permute-start.1 = (f32[32,80,128]{2,1,0:T(8,128)S(1)}, f32[32,80,128]{2,1,0:T(8,128)S(1)}, u32[]{:S(2)}, u32[]{:S(2)}) collective-permute-start(f32[32,80,128]{2,1,0:T(8,128)S(1)} %get-tuple-element.12), channel_id=1, source_target_pairs={{0,8},{1,9},{2,10},{3,11},{4,12},{5,13},{6,14},{7,15},{8,0},{9,1},... | collective-permute-start | bytes 3932168 | tf_op jit(solution)/shard_map/ppermute | solution.py:355

commit v3 on v2

--- a/solution.py
+++ b/solution.py
@@ -14,10 +14,11 @@
 OWN = 16
 WIN = 32
 ROWS = WIN + 3 * OWN
-STEP = 8
+STEP = 16
 SPLITS = ()
-NEAR = 1
-LOAD = 8
+NEAR = 2
+HALO_CUTS = (0, 16, 32, 48, 64)
+LOAD = 16
 AHEAD = 3
 LIMITS = (54, 46, 32)
 F32 = jnp.float32
@@ -130,44 +131,54 @@
 
 def halo_kernel(number, *refs, cuts):
     source, (out, held), small = refs[:6], refs[6:8], refs[8:14]
-    full, pick, func, load_sem, small_sem = refs[14:]
+    full, pick, func, made, load_sem, small_sem, store_sem = refs[14:]
     sends, kernel, growth, rate, target, table = small
+    stores = []
+    copies = copy_all((*source[:5], source[5].at[0:2]), small, small_sem)
     loads = start_loads(number, held, load_sem, cuts)
-    copies = copy_all((*source[:5], source[5].at[0:2]), small, small_sem)
+    for copy in copies:
+        copy.wait()
     for copy in loads[1:AHEAD]:
         copy.start()
-    for copy in copies:
-        copy.wait()
 
     _, partner, odd = place()
     fill_functionals(full, kernel, growth, rate, target, table)
     func[...] = functionals(full, partner)
-    pick[...] = pick_two(jnp.where(odd == 1, sends[0:1, :], sends[1:2, :]))
+    sent = jnp.where(odd == 1, sends[0:1, :], sends[1:2, :])
+    named = jnp.broadcast_to(jnp.concatenate([sent, sent], axis=1), (PIV, 2 * SLOTS))
+    lane, upper = lax.rem(named, PIV), named >= PIV
+    even = iota((PIV, 2 * SLOTS), 1) < SLOTS
 
     for i, (start, stop) in enumerate(zip(cuts, cuts[1:])):
         loads[i].wait()
         if i + AHEAD < len(loads):
             loads[i + AHEAD].start()
-        for s in range(start - cuts[0], stop - cuts[0], STEP):
-            both = jnp.concatenate(
-                [
-                    jnp.concatenate([held[s + 2 * q], held[s + 2 * q + 1]], axis=1)
-                    for q in range(STEP // 2)
-                ],
-                axis=0,
+        s, pairs = start - cuts[0], (stop - start) // 2
+        def taken(l):
+            x = held[s + l]
+            a = jnp.take_along_axis(x[:, :PIV], lane, axis=1)
+            b = jnp.take_along_axis(x[:, PIV:], lane, axis=1)
+            return jnp.where(upper, b, a)
+
+        got_hi, got_lo = split(
+            jnp.concatenate(
+                [jnp.where(even, taken(2 * q), taken(2 * q + 1)) for q in range(pairs)], axis=0
             )
-            hi, lo = split(both)
-            got_hi = dot(hi, pick[...]).astype(BF16)
-            got_lo = dot(lo, pick[...]).astype(BF16)
-            for q in range(0, STEP // 2, 2):
-                a, b = slice(q * PIV, (q + 1) * PIV), slice((q + 1) * PIV, (q + 2) * PIV)
-                got = apply(
-                    func[...],
-                    jnp.concatenate([got_hi[a], got_hi[b]], axis=1),
-                    jnp.concatenate([got_lo[a], got_lo[b]], axis=1),
-                )
-                out[s // 2 + q] = got[:, 0 : 2 * SLOTS]
-                out[s // 2 + q + 1] = got[:, 2 * SLOTS :]
+        )
+        for q in range(0, pairs, 2):
+            a, b = slice(q * PIV, (q + 1) * PIV), slice((q + 1) * PIV, (q + 2) * PIV)
+            got = apply(
+                func[...],
+                jnp.concatenate([got_hi[a], got_hi[b]], axis=1),
+                jnp.concatenate([got_lo[a], got_lo[b]], axis=1),
+            )
+            made[s // 2 + q] = got[:, 0 : 2 * SLOTS]
+            made[s // 2 + q + 1] = got[:, 2 * SLOTS :]
+        rows = pl.ds(s // 2, pairs)
+        stores.append(pltpu.make_async_copy(made.at[rows], out.at[rows], store_sem.at[i]))
+        stores[-1].start()
+    for copy in stores:
+        copy.wait()
 
 
 def local_kernel(number, *refs, cuts):
@@ -193,18 +204,20 @@
         total = total + jnp.where(neighbours[e : e + 1, :] == row, m[e : e + 1], 0.0)
     mixing[0], mixing[1] = split(total)
 
-    row = iota((4 * SLOTS, COLS), 0)
-    inner = lax.rem(row, 2 * SLOTS)
-    upper = jnp.where(row < 2 * SLOTS, 1 - odd, odd)
-    for a in range(2):
-        slot = COLS + upper * SLOTS + inner - a * SLOTS
-        slot = jnp.where((inner >= a * SLOTS) & (inner < (a + 1) * SLOTS), slot, -1)
-        total = jnp.zeros((4 * SLOTS, COLS), F32)
-        for e in range(3):
-            total = total + jnp.where(neighbours[e : e + 1, :] == slot, m[e : e + 1], 0.0)
-        hi, lo = split(total)
-        came[0, :, a * COLS : (a + 1) * COLS] = hi
-        came[1, :, a * COLS : (a + 1) * COLS] = lo
+    row = iota((2 * SLOTS, COLS), 0)
+    for way in range(2):
+        upper = 1 - odd if way == 0 else odd
+        for a in range(2):
+            slot = COLS + upper * SLOTS + row - a * SLOTS
+            slot = jnp.where((row >= a * SLOTS) & (row < (a + 1) * SLOTS), slot, -1)
+            total = jnp.zeros((2 * SLOTS, COLS), F32)
+            for e in range(3):
+                total = total + jnp.where(neighbours[e : e + 1, :] == slot, m[e : e + 1], 0.0)
+            hi, lo = split(total)
+            lanes = slice(a * COLS, (a + 1) * COLS)
+            came[way, 0 : 2 * SLOTS, lanes] = hi
+            came[way, 2 * SLOTS : 4 * SLOTS, lanes] = hi
+            came[way, 4 * SLOTS :, lanes] = lo
     sym = symmetric(kernel)
     start = pl.multiple_of(rank * OWN, OWN)
     shift = lax.rem(PIV + (WIN - OWN) - rank * OWN, PIV)
@@ -238,29 +251,33 @@
             near[s // 2 // piece][at : at + pairs] = got.reshape(pairs, ROWS, 2 * SLOTS)
 
 
-def update_kernel(base, came, band, far, *rest, first):
-    near = rest[:NEAR]
+def spread(message, came):
+    hi, lo = split(message)
+    return dot(jnp.concatenate([hi, lo], axis=1), came[0 : 4 * SLOTS]) + dot(hi, came[4 * SLOTS :])
+
+
+def near_kernel(base, came, *refs):
+    *near, out = refs
+    count = STEP // 2 * ROWS
     piece = near[0].shape[0]
-    out, done, store_sem = rest[-3:]
-    pairs = STEP // 2
-    own = WIN - OWN
-    stores = []
-    for i, s in enumerate(range(0, done.shape[0], STEP)):
-        both = jnp.concatenate(
-            [
-                jnp.concatenate(
-                    [near[(first + s) // 2 // piece][(first + s) // 2 % piece + q], far[s // 2 + q]],
-                    axis=1,
-                )
-                for q in range(pairs)
-            ],
-            axis=0,
-        )
-        hi, lo = split(both)
-        got = dot(hi, came[0]) + dot(lo, came[0]) + dot(hi, came[1])
+    for s in range(0, base.shape[0], STEP):
+        at = s // 2 % piece
+        part = near[s // 2 // piece][at : at + STEP // 2]
+        got = spread(part.reshape(count, 2 * SLOTS), came[0])
         for l in range(STEP):
             q, a = l // 2, l % 2
-            v = base[first + s + l] + got[q * ROWS : (q + 1) * ROWS, a * COLS : (a + 1) * COLS]
+            out[s + l] = base[s + l] + got[q * ROWS : (q + 1) * ROWS, a * COLS : (a + 1) * COLS]
+
+
+def update_kernel(base, came, band, far, out, done, store_sem):
+    own = WIN - OWN
+    count = STEP // 2 * ROWS
+    stores = []
+    for i, s in enumerate(range(0, base.shape[0], STEP)):
+        got = spread(far[s // 2 : (s + STEP) // 2].reshape(count, 2 * SLOTS), came[1])
+        for l in range(STEP):
+            q, a = l // 2, l % 2
+            v = base[s + l] + got[q * ROWS : (q + 1) * ROWS, a * COLS : (a + 1) * COLS]
             window = v[0:WIN]
             n_hi, n_lo = split(window)
             births = dot(band[...], jnp.concatenate([n_hi, n_lo, n_hi], axis=0))
@@ -269,11 +286,8 @@
             for m in range(2, 5):
                 total = total + window[own - m : WIN - m] * births[(m - 2) * OWN : (m - 1) * OWN]
             done[s + l] = total
-        stores.append(
-            pltpu.make_async_copy(
-                done.at[pl.ds(s, STEP)], out.at[pl.ds(first + s, STEP)], store_sem.at[i]
-            )
-        )
+        rows = pl.ds(s, STEP)
+        stores.append(pltpu.make_async_copy(done.at[rows], out.at[rows], store_sem.at[i]))
         stores[-1].start()
     for copy in stores:
         copy.wait()
@@ -309,11 +323,11 @@
 
     far = []
     for first, last in zip((0,) + SPLITS, SPLITS + (levels,)):
-        cuts = tuple(range(first, last + 1, LOAD))
+        cuts = HALO_CUTS
         message = pl.pallas_call(
             functools.partial(halo_kernel, cuts=cuts),
             in_specs=[hbm] * 7,
-            out_specs=vmem,
+            out_specs=hbm,
             out_shape=shape(((last - first) // 2, ROWS, 2 * SLOTS), F32),
             scratch_shapes=[pltpu.VMEM((last - first, PIV, COLS), F32)]
             + scratch(halo_small[:5] + (table[0:2],))
@@ -321,8 +335,10 @@
                 pltpu.VMEM((3, PIV, PIV), F32),
                 pltpu.VMEM((2 * COLS, 2 * SLOTS), BF16),
                 pltpu.VMEM((ROWS + 3 * OWN, 2 * PIV), BF16),
+                pltpu.VMEM(((last - first) // 2, ROWS, 2 * SLOTS), F32),
                 pltpu.SemaphoreType.DMA((len(cuts) - 1,)),
                 pltpu.SemaphoreType.DMA((6,)),
+                pltpu.SemaphoreType.DMA((len(cuts) - 1,)),
             ],
             compiler_params=params(LIMITS[0]),
             cost_estimate=cost,
@@ -337,7 +353,7 @@
         out_specs=[vmem] * (3 + NEAR),
         out_shape=[shape((levels, ROWS, COLS), F32)]
         + [shape((levels // 2 // NEAR, ROWS, 2 * SLOTS), F32)] * NEAR
-        + [shape((2, 4 * SLOTS, 2 * COLS), BF16), shape((3 * OWN, 3 * WIN), BF16)],
+        + [shape((2, 6 * SLOTS, 2 * COLS), BF16), shape((3 * OWN, 3 * WIN), BF16)],
         scratch_shapes=[pltpu.VMEM(number.shape, F32)]
         + scratch(small)
         + [
@@ -354,26 +370,30 @@
     )(number, *small)
     near = [lax.ppermute(x, ("cells", "pairs"), near_pairs) for x in near]
 
-    out = ()
-    for first, message in far:
-        count = 2 * message.shape[0]
-        out = (
-            pl.pallas_call(
-                functools.partial(update_kernel, first=first),
-                in_specs=[vmem] * (4 + NEAR) + [hbm] * len(out),
-                out_specs=hbm,
-                out_shape=shape((levels, OWN, COLS), F32),
-                input_output_aliases={4 + NEAR: 0} if out else {},
-                scratch_shapes=[
-                    pltpu.VMEM((count, OWN, COLS), F32),
-                    pltpu.SemaphoreType.DMA((count // STEP,)),
-                ],
-                compiler_params=params(LIMITS[2]),
-                cost_estimate=cost,
-                name=f"update{first}",
-            )(base, came, band, message, *near, *out),
-        )
-    return out[0]
+    base = pl.pallas_call(
+        near_kernel,
+        in_specs=[vmem] * (2 + NEAR),
+        out_specs=vmem,
+        out_shape=shape(base.shape, F32),
+        input_output_aliases={0: 0},
+        compiler_params=params(LIMITS[2]),
+        cost_estimate=cost,
+        name="near",
+    )(base, came, *near)
+    [(_, message)] = far
+    return pl.pallas_call(
+        update_kernel,
+        in_specs=[vmem] * 4,
+        out_specs=hbm,
+        out_shape=shape((levels, OWN, COLS), F32),
+        scratch_shapes=[
+            pltpu.VMEM((levels, OWN, COLS), F32),
+            pltpu.SemaphoreType.DMA((levels // STEP,)),
+        ],
+        compiler_params=params(LIMITS[2]),
+        cost_estimate=cost,
+        name="update",
+    )(base, came, band, message)
 
 
 def solution(mesh):

time: 34.2 us -> 30.5 us (0.89)
  Pallas kernels: 20.9 us -> 18.3 us
  waiting for transfers between devices: 9.99 us -> 9.13 us
    ppermute x1, waiting for transfers between devices: 9.98 us -> 6.56 us  [on_device(): far.append((first, lax.ppermute(message, ('cells', 'pairs'), far_pairs)))]
    ppermute x1 -> x2, waiting for transfers between devices: 0.01 us -> 2.57 us  [on_device(): near = [lax.ppermute(x, ('cells', 'pairs'), near_pairs) for x in near]]
    pallas_call x1, Pallas kernels: 8.03 us -> 5.97 us  [on_device(): pl.pallas_call(functools.partial(halo_kernel, cuts=cuts), in_specs=[hbm]...]
    pallas_call x1, Pallas kernels: 8.31 us -> 7.51 us  [on_device(): pl.pallas_call(functools.partial(local_kernel, cuts=cuts), in_specs=[hbm]...]
    pallas_call x1 -> x2, Pallas kernels: 4.56 us -> 4.8 us  [the longest x1 3.06 us: on_device(): pl.pallas_call(update_kernel, in_specs=[vmem] * 4, out_specs=hbm, out_sha...]
    ppermute x1 -> x2, starting transfers between devices: 0.84 us -> 0.75 us  [on_device(): near = [lax.ppermute(x, ('cells', 'pairs'), near_pairs) for x in near]]
  transfers between devices with their start and end apart: 2 -> 3, of which waited for: 1 -> 3; matrix products, arithmetic and copies ran while one was open for 0% -> 0% of each run, Pallas kernels for 24% -> 31%
where the time goes in v3:
time: 30.5 us; the launch traced here: 30.3 us
  Pallas kernels  18.3 us (60%)
  waiting for transfers between devices  9.13 us (30%)
  starting transfers between devices  2.76 us (9%)
    pallas_call x1, Pallas kernels, on_device(): pl.pallas_call(functools.partial(local_kernel, cuts=cuts), in_specs=[hbm]...  7.51 us
    ppermute x1, waiting for transfers between devices, on_device(): far.append((first, lax.ppermute(message, ('cells', 'pairs'), far_pairs)))  6.56 us
    pallas_call x1, Pallas kernels, on_device(): pl.pallas_call(functools.partial(halo_kernel, cuts=cuts), in_specs=[hbm]...  5.97 us
    pallas_call x1, Pallas kernels, on_device(): pl.pallas_call(update_kernel, in_specs=[vmem] * 4, out_specs=hbm, out_sha...  3.06 us
    ppermute x2, waiting for transfers between devices, on_device(): near = [lax.ppermute(x, ('cells', 'pairs'), near_pairs) for x in near]  2.57 us
    ppermute x1, starting transfers between devices, on_device(): far.append((first, lax.ppermute(message, ('cells', 'pairs'), far_pairs)))  2.02 us
    pallas_call x1, Pallas kernels, on_device(): pl.pallas_call(near_kernel, in_specs=[vmem] * (2 + NEAR), out_specs=vmem,...  1.74 us
    ppermute x2, starting transfers between devices, on_device(): near = [lax.ppermute(x, ('cells', 'pairs'), near_pairs) for x in near]  0.75 us
  transfers between devices with their start and end apart: 3, of which 3 were waited for; matrix products, arithmetic and copies ran while one was open for 0% of the time, Pallas kernels for 31%

profile of v3, /device:TPU:101, one launch (start us, length us, event | category | flops | bytes accessed | tf_op | source)
XLA Modules:
  0.0 30.3 jit_solution(14126891238988579412)
XLA Ops:
  0.0 0.0 copy-start
  0.0 0.0 copy-start.6
  0.0 0.0 copy-start.7
  0.0 0.0 copy-start.4
  0.0 0.0 copy-start.1
  0.0 0.0 copy-start.5
  0.0 0.0 copy-start.2
  0.0 0.0 copy-start.3
  0.1 6.0 %halo0.1 = f32[32,80,128]{2,1,0:T(8,128)} custom-call(f32[64,128,256]{2,1,0:T(8,128)} %number.3, s32[2,64]{1,0:T(2,128)} %refs_0_.3, f32[128,128]{1,0:T(8,128)} %refs_1_.3, f32[1,128]{1,0:T(1,128)} %bitcast.2, f32[1,128]{1,0:T(1,128)} %bitcast.4, s32[2,128]{1,0:T(2,128)} %refs_4_.1, f32[5,128,128]{2,1,0:T(8,128)} %constant.2.clone.refs_7_.refs_5_), custom_call_target="tpu_custom_call" | custom-call | flops 1000000 | bytes 1000000 | tf_op jit(solution)/shard_map/halo0/pallas_call | solution.py:327
  6.0 2.0 %collective-permute-start.2 = (f32[32,80,128]{2,1,0:T(8,128)}, f32[32,80,128]{2,1,0:T(8,128)S(1)}, u32[]{:S(2)}, u32[]{:S(2)}) collective-permute-start(f32[32,80,128]{2,1,0:T(8,128)} %halo0.1), channel_id=1, source_target_pairs={{8,16},{9,17},{10,18},{11,19},{12,20},{13,21},{14,22},{15,23},{16,... | collective-permute-start | bytes 3932168 | tf_op jit(solution)/shard_map/ppermute | solution.py:347
  8.1 0.0 copy-done
  8.1 0.0 copy-done.6
  8.1 0.0 copy-done.7
  8.1 0.0 copy-done.4
  8.1 0.0 copy-done.1
  8.1 0.0 copy-done.5
  8.1 0.0 copy-done.2
  8.1 0.0 copy-done.3
  8.1 7.5 %local.1 = (f32[64,80,256]{2,1,0:T(8,128)S(1)}, f32[16,80,128]{2,1,0:T(8,128)S(1)}, f32[16,80,128]{2,1,0:T(8,128)S(1)}, bf16[2,384,512]{2,1,0:T(8,128)(2,1)S(1)}, bf16[48,96]{1,0:T(8,128)(2,1)S(1)}) custom-call(f32[64,128,256]{2,1,0:T(8,128)} %number.3, s32[2,64]{1,0:T(2,128)S(1)} %copy-done.4, f32[3,256]{1,0:T(4,128)S(1)} %copy-done.2, ...), custom_call_target="tpu_custom_call" | custom-call | flops 1000000 | bytes 1000000 | tf_op jit(solution)/shard_map/local/pallas_call | solution.py:350
  15.7 0.7 %collective-permute-start = (f32[16,80,128]{2,1,0:T(8,128)S(1)}, f32[16,80,128]{2,1,0:T(8,128)S(1)}, u32[]{:S(2)}, u32[]{:S(2)}) collective-permute-start(f32[16,80,128]{2,1,0:T(8,128)S(1)} %get-tuple-element.12), channel_id=1, source_target_pairs={{0,8},{1,9},{2,10},{3,11},{4,12},{5,13},{6,14},{7,15},{8,0},{9,1},... | collective-permute-start | bytes 1966088 | tf_op jit(solution)/shard_map/ppermute | solution.py:371
  16.3 0.1 collective-permute-start.1
  16.4 1.6 %collective-permute-done.refs_0_ = f32[16,80,128]{2,1,0:T(8,128)S(1)} collective-permute-done((f32[16,80,128]{2,1,0:T(8,128)S(1)}, f32[16,80,128]{2,1,0:T(8,128)S(1)}, u32[]{:S(2)}, u32[]{:S(2)}) %collective-permute-start) | collective-permute-done | bytes 655392 | tf_op jit(solution)/shard_map/ppermute | solution.py:371
  18.0 0.9 %collective-permute-done.1.refs_1_ = f32[16,80,128]{2,1,0:T(8,128)S(1)} collective-permute-done((f32[16,80,128]{2,1,0:T(8,128)S(1)}, f32[16,80,128]{2,1,0:T(8,128)S(1)}, u32[]{:S(2)}, u32[]{:S(2)}) %collective-permute-start.1) | collective-permute-done | bytes 655392 | tf_op jit(solution)/shard_map/ppermute | solution.py:371
  19.0 1.7 %near.1.base = f32[64,80,256]{2,1,0:T(8,128)S(1)} custom-call(f32[64,80,256]{2,1,0:T(8,128)S(1)} %get-tuple-element.10.base, bf16[2,384,512]{2,1,0:T(8,128)(2,1)S(1)} %get-tuple-element.11.came, f32[16,80,128]{2,1,0:T(8,128)S(1)} %collective-permute-done.refs_0_, f32[16,80,128]{2,1,0:T(8,128)S(1)} %collective-permute-done.1.refs_1_), custom_call_target="tpu_custom_call", output_to_operand_aliasing={{}: (0, {})} | custom-call | flops 1000000 | bytes 1000000 | tf_op jit(solution)/shard_map/near/pallas_call | solution.py:373
  20.7 6.6 %collective-permute-done.2.far = f32[32,80,128]{2,1,0:T(8,128)S(1)} collective-permute-done((f32[32,80,128]{2,1,0:T(8,128)}, f32[32,80,128]{2,1,0:T(8,128)S(1)}, u32[]{:S(2)}, u32[]{:S(2)}) %collective-permute-start.2) | collective-permute-done | bytes 1310752 | tf_op jit(solution)/shard_map/ppermute | solution.py:347
  27.3 3.1 %update.1 = f32[64,16,256]{2,1,0:T(8,128)} custom-call(f32[64,80,256]{2,1,0:T(8,128)S(1)} %near.1.base, bf16[2,384,512]{2,1,0:T(8,128)(2,1)S(1)} %get-tuple-element.11.came, bf16[48,96]{1,0:T(8,128)(2,1)S(1)} %get-tuple-element.14.band, f32[32,80,128]{2,1,0:T(8,128)S(1)} %collective-permute-done.2.far), custom_call_target="tpu_custom_call" | custom-call | flops 1000000 | bytes 1000000 | tf_op jit(solution)/shard_map/update/pallas_call | solution.py:384
Async XLA Ops:
  0.0 8.1 %copy-start = (f32[5,128,128]{2,1,0:T(8,128)S(1)}, f32[5,128,128]{2,1,0:T(8,128)}, u32[]{:S(2)}) copy-start(f32[5,128,128]{2,1,0:T(8,128)} %constant.2.clone.refs_7_.refs_5_) | copy-start | bytes 983044
  0.0 8.1 %copy-start.6 = (f32[128]{0:T(128)S(1)}, f32[128]{0:T(128)}, u32[]{:S(2)}) copy-start(f32[128]{0:T(128)} %param.14) | copy-start | bytes 1540
  0.0 8.1 %copy-start.7 = (f32[128]{0:T(128)S(1)}, f32[128]{0:T(128)}, u32[]{:S(2)}) copy-start(f32[128]{0:T(128)} %param.15) | copy-start | bytes 1540
  0.0 8.1 %copy-start.4 = (s32[2,64]{1,0:T(2,128)S(1)}, s32[2,64]{1,0:T(2,128)}, u32[]{:S(2)}) copy-start(s32[2,64]{1,0:T(2,128)} %refs_0_.3) | copy-start | bytes 1540
  0.0 8.1 %copy-start.1 = (f32[128,128]{1,0:T(8,128)S(1)}, f32[128,128]{1,0:T(8,128)}, u32[]{:S(2)}) copy-start(f32[128,128]{1,0:T(8,128)} %refs_1_.3) | copy-start | bytes 196612
  0.0 8.1 %copy-start.5 = (s32[2,128]{1,0:T(2,128)S(1)}, s32[2,128]{1,0:T(2,128)}, u32[]{:S(2)}) copy-start(s32[2,128]{1,0:T(2,128)} %refs_4_.1) | copy-start | bytes 3076
  0.0 8.1 %copy-start.2 = (f32[3,256]{1,0:T(4,128)S(1)}, f32[3,256]{1,0:T(4,128)}, u32[]{:S(2)}) copy-start(f32[3,256]{1,0:T(4,128)} %refs_1_.2) | copy-start | bytes 9220
  0.0 8.1 %copy-start.3 = (s32[3,256]{1,0:T(4,128)S(1)}, s32[3,256]{1,0:T(4,128)}, u32[]{:S(2)}) copy-start(s32[3,256]{1,0:T(4,128)} %refs_2_.1) | copy-start | bytes 9220
  6.0 21.2 %collective-permute-start.2 = (f32[32,80,128]{2,1,0:T(8,128)}, f32[32,80,128]{2,1,0:T(8,128)S(1)}, u32[]{:S(2)}, u32[]{:S(2)}) collective-permute-start(f32[32,80,128]{2,1,0:T(8,128)} %halo0.1), channel_id=1, source_target_pairs={{8,16},{9,17},{10,18},{11,19},{12,20},{13,21},{14,22},{15,23},{16,... | collective-permute-start | bytes 3932168 | tf_op jit(solution)/shard_map/ppermute | solution.py:347
  15.7 2.4 %collective-permute-start = (f32[16,80,128]{2,1,0:T(8,128)S(1)}, f32[16,80,128]{2,1,0:T(8,128)S(1)}, u32[]{:S(2)}, u32[]{:S(2)}) collective-permute-start(f32[16,80,128]{2,1,0:T(8,128)S(1)} %get-tuple-element.12), channel_id=1, source_target_pairs={{0,8},{1,9},{2,10},{3,11},{4,12},{5,13},{6,14},{7,15},{8,0},{9,1},... | collective-permute-start | bytes 1966088 | tf_op jit(solution)/shard_map/ppermute | solution.py:371
  16.3 2.7 %collective-permute-start.1 = (f32[16,80,128]{2,1,0:T(8,128)S(1)}, f32[16,80,128]{2,1,0:T(8,128)S(1)}, u32[]{:S(2)}, u32[]{:S(2)}) collective-permute-start(f32[16,80,128]{2,1,0:T(8,128)S(1)} %get-tuple-element.13), channel_id=1, source_target_pairs={{0,8},{1,9},{2,10},{3,11},{4,12},{5,13},{6,14},{7,15},{8,0},{9,1},... | collective-permute-start | bytes 1966088 | tf_op jit(solution)/shard_map/ppermute | solution.py:371

commit v4 on v3

--- a/solution.py
+++ b/solution.py
@@ -172,9 +172,8 @@
                 jnp.concatenate([got_hi[a], got_hi[b]], axis=1),
                 jnp.concatenate([got_lo[a], got_lo[b]], axis=1),
             )
-            made[s // 2 + q] = got[:, 0 : 2 * SLOTS]
-            made[s // 2 + q + 1] = got[:, 2 * SLOTS :]
-        rows = pl.ds(s // 2, pairs)
+            made[s // 4 + q // 2] = pack(got[:, 0 : 2 * SLOTS], got[:, 2 * SLOTS :])
+        rows = pl.ds(s // 4, pairs // 2)
         stores.append(pltpu.make_async_copy(made.at[rows], out.at[rows], store_sem.at[i]))
         stores[-1].start()
     for copy in stores:
@@ -207,17 +206,16 @@
     row = iota((2 * SLOTS, COLS), 0)
     for way in range(2):
         upper = 1 - odd if way == 0 else odd
+        slot = COLS + upper * SLOTS + lax.rem(row, SLOTS)
+        total = jnp.zeros((2 * SLOTS, COLS), F32)
+        for e in range(3):
+            total = total + jnp.where(neighbours[e : e + 1, :] == slot, m[e : e + 1], 0.0)
+        hi = total.astype(BF16)
+        low = total - hi.astype(F32)
         for a in range(2):
-            slot = COLS + upper * SLOTS + row - a * SLOTS
-            slot = jnp.where((row >= a * SLOTS) & (row < (a + 1) * SLOTS), slot, -1)
-            total = jnp.zeros((2 * SLOTS, COLS), F32)
-            for e in range(3):
-                total = total + jnp.where(neighbours[e : e + 1, :] == slot, m[e : e + 1], 0.0)
-            hi, lo = split(total)
-            lanes = slice(a * COLS, (a + 1) * COLS)
-            came[way, 0 : 2 * SLOTS, lanes] = hi
-            came[way, 2 * SLOTS : 4 * SLOTS, lanes] = hi
-            came[way, 4 * SLOTS :, lanes] = lo
+            came[way, a, 0 : 2 * SLOTS] = hi
+            there = (row >= a * SLOTS) & (row < (a + 1) * SLOTS)
+            came[way, a, 2 * SLOTS :] = jnp.where(there, low, 0.0).astype(BF16)
     sym = symmetric(kernel)
     start = pl.multiple_of(rank * OWN, OWN)
     shift = lax.rem(PIV + (WIN - OWN) - rank * OWN, PIV)
@@ -252,8 +250,15 @@
 
 
 def spread(message, came):
-    hi, lo = split(message)
-    return dot(jnp.concatenate([hi, lo], axis=1), came[0 : 4 * SLOTS]) + dot(hi, came[4 * SLOTS :])
+    hi = message.astype(BF16)
+    high = hi.astype(F32)
+    turned = pltpu.roll(message - high, SLOTS, 1)
+    left = iota(message.shape, 1) < SLOTS
+    first = jnp.where(left, high, turned).astype(BF16)
+    second = jnp.where(left, turned, high).astype(BF16)
+    return [
+        dot(jnp.concatenate([part, hi], axis=1), came[a]) for a, part in enumerate((first, second))
+    ]
 
 
 def near_kernel(base, came, *refs):
@@ -266,18 +271,29 @@
         got = spread(part.reshape(count, 2 * SLOTS), came[0])
         for l in range(STEP):
             q, a = l // 2, l % 2
-            out[s + l] = base[s + l] + got[q * ROWS : (q + 1) * ROWS, a * COLS : (a + 1) * COLS]
+            out[s + l] = base[s + l] + got[a][q * ROWS : (q + 1) * ROWS]
+
+
+def pack(a, b):
+    mixed = jnp.where(iota((8, 2 * SLOTS), 0) < 4, pltpu.roll(b[0:8], 4, 0), a[0:8])
+    return jnp.concatenate([a[8:], b[8:], mixed], axis=0)
+
+
+def unpack(m):
+    cut = ROWS - 8
+    mixed = m[2 * cut :]
+    return jnp.concatenate([mixed, m[0:cut], pltpu.roll(mixed, 4, 0), m[cut : 2 * cut]], axis=0)
 
 
 def update_kernel(base, came, band, far, out, done, store_sem):
     own = WIN - OWN
-    count = STEP // 2 * ROWS
     stores = []
     for i, s in enumerate(range(0, base.shape[0], STEP)):
-        got = spread(far[s // 2 : (s + STEP) // 2].reshape(count, 2 * SLOTS), came[1])
+        part = [unpack(far[q]) for q in range(s // 4, (s + STEP) // 4)]
+        got = spread(jnp.concatenate(part, axis=0), came[1])
         for l in range(STEP):
             q, a = l // 2, l % 2
-            v = base[s + l] + got[q * ROWS : (q + 1) * ROWS, a * COLS : (a + 1) * COLS]
+            v = base[s + l] + got[a][q * ROWS : (q + 1) * ROWS]
             window = v[0:WIN]
             n_hi, n_lo = split(window)
             births = dot(band[...], jnp.concatenate([n_hi, n_lo, n_hi], axis=0))
@@ -328,14 +344,14 @@
             functools.partial(halo_kernel, cuts=cuts),
             in_specs=[hbm] * 7,
             out_specs=hbm,
-            out_shape=shape(((last - first) // 2, ROWS, 2 * SLOTS), F32),
+            out_shape=shape(((last - first) // 4, 2 * ROWS - 8, 2 * SLOTS), F32),
             scratch_shapes=[pltpu.VMEM((last - first, PIV, COLS), F32)]
             + scratch(halo_small[:5] + (table[0:2],))
             + [
                 pltpu.VMEM((3, PIV, PIV), F32),
                 pltpu.VMEM((2 * COLS, 2 * SLOTS), BF16),
                 pltpu.VMEM((ROWS + 3 * OWN, 2 * PIV), BF16),
-                pltpu.VMEM(((last - first) // 2, ROWS, 2 * SLOTS), F32),
+                pltpu.VMEM(((last - first) // 4, 2 * ROWS - 8, 2 * SLOTS), F32),
                 pltpu.SemaphoreType.DMA((len(cuts) - 1,)),
                 pltpu.SemaphoreType.DMA((6,)),
                 pltpu.SemaphoreType.DMA((len(cuts) - 1,)),
@@ -353,7 +369,7 @@
         out_specs=[vmem] * (3 + NEAR),
         out_shape=[shape((levels, ROWS, COLS), F32)]
         + [shape((levels // 2 // NEAR, ROWS, 2 * SLOTS), F32)] * NEAR
-        + [shape((2, 6 * SLOTS, 2 * COLS), BF16), shape((3 * OWN, 3 * WIN), BF16)],
+        + [shape((2, 2, 4 * SLOTS, COLS), BF16), shape((3 * OWN, 3 * WIN), BF16)],
         scratch_shapes=[pltpu.VMEM(number.shape, F32)]
         + scratch(small)
         + [

time: 30.5 us -> 29.4 us (0.964)
  Pallas kernels: 18.3 us -> 17.3 us
    pallas_call x1, Pallas kernels: 1.74 us -> 1.15 us  [on_device(): pl.pallas_call(near_kernel, in_specs=[vmem] * (2 + NEAR), out_specs=vmem,...]
    pallas_call x1, Pallas kernels: 3.06 us -> 2.71 us  [on_device(): pl.pallas_call(update_kernel, in_specs=[vmem] * 4, out_specs=hbm, out_sha...]
  transfers between devices with their start and end apart: 3 -> 3, of which waited for: 3 -> 3; matrix products, arithmetic and copies ran while one was open for 0% -> 0% of each run, Pallas kernels for 31% -> 30%
where the time goes in v4:
time: 29.4 us; the launch traced here: 29.3 us
  Pallas kernels  17.3 us (59%)
  waiting for transfers between devices  9.01 us (31%)
  starting transfers between devices  2.76 us (9%)
    pallas_call x1, Pallas kernels, on_device(): pl.pallas_call(functools.partial(local_kernel, cuts=cuts), in_specs=[hbm]...  7.52 us
    ppermute x1, waiting for transfers between devices, on_device(): far.append((first, lax.ppermute(message, ('cells', 'pairs'), far_pairs)))  6.44 us
    pallas_call x1, Pallas kernels, on_device(): pl.pallas_call(functools.partial(halo_kernel, cuts=cuts), in_specs=[hbm]...  5.95 us
    pallas_call x1, Pallas kernels, on_device(): pl.pallas_call(update_kernel, in_specs=[vmem] * 4, out_specs=hbm, out_sha...  2.71 us
    ppermute x2, waiting for transfers between devices, on_device(): near = [lax.ppermute(x, ('cells', 'pairs'), near_pairs) for x in near]  2.57 us
    ppermute x1, starting transfers between devices, on_device(): far.append((first, lax.ppermute(message, ('cells', 'pairs'), far_pairs)))  2.02 us
    pallas_call x1, Pallas kernels, on_device(): pl.pallas_call(near_kernel, in_specs=[vmem] * (2 + NEAR), out_specs=vmem,...  1.15 us
    ppermute x2, starting transfers between devices, on_device(): near = [lax.ppermute(x, ('cells', 'pairs'), near_pairs) for x in near]  0.74 us
  transfers between devices with their start and end apart: 3, of which 3 were waited for; matrix products, arithmetic and copies ran while one was open for 0% of the time, Pallas kernels for 30%

profile of v4, /device:TPU:101, one launch (start us, length us, event | category | flops | bytes accessed | tf_op | source)
XLA Modules:
  0.0 29.3 jit_solution(1247218971202997561)
XLA Ops:
  0.0 0.0 copy-start
  0.0 0.0 copy-start.6
  0.0 0.0 copy-start.7
  0.0 0.0 copy-start.4
  0.0 0.0 copy-start.1
  0.0 0.0 copy-start.5
  0.0 0.0 copy-start.2
  0.0 0.0 copy-start.3
  0.1 5.9 %halo0.1 = f32[16,152,128]{2,1,0:T(8,128)} custom-call(f32[64,128,256]{2,1,0:T(8,128)} %number.3, s32[2,64]{1,0:T(2,128)} %refs_0_.3, f32[128,128]{1,0:T(8,128)} %refs_1_.3, f32[1,128]{1,0:T(1,128)} %bitcast.2, f32[1,128]{1,0:T(1,128)} %bitcast.4, s32[2,128]{1,0:T(2,128)} %refs_4_.1, f32[5,128,128]{2,1,0:T(8,128)} %constant.2.clone.refs_7_.refs_5_), custom_call_target="tpu_custom_call" | custom-call | flops 1000000 | bytes 1000000 | tf_op jit(solution)/shard_map/halo0/pallas_call | solution.py:343
  6.0 2.0 %collective-permute-start.2 = (f32[16,152,128]{2,1,0:T(8,128)}, f32[16,152,128]{2,1,0:T(8,128)S(1)}, u32[]{:S(2)}, u32[]{:S(2)}) collective-permute-start(f32[16,152,128]{2,1,0:T(8,128)} %halo0.1), channel_id=1, source_target_pairs={{8,16},{9,17},{10,18},{11,19},{12,20},{13,21},{14,22},{15,23},{16,... | collective-permute-start | bytes 3735560 | tf_op jit(solution)/shard_map/ppermute | solution.py:363
  8.0 0.0 copy-done
  8.1 0.0 copy-done.6
  8.1 0.0 copy-done.7
  8.1 0.0 copy-done.4
  8.1 0.0 copy-done.1
  8.1 0.0 copy-done.5
  8.1 0.0 copy-done.2
  8.1 0.0 copy-done.3
  8.1 7.5 %local.1 = (f32[64,80,256]{2,1,0:T(8,128)S(1)}, f32[16,80,128]{2,1,0:T(8,128)S(1)}, f32[16,80,128]{2,1,0:T(8,128)S(1)}, bf16[2,2,256,256]{3,2,1,0:T(8,128)(2,1)S(1)}, bf16[48,96]{1,0:T(8,128)(2,1)S(1)}) custom-call(f32[64,128,256]{2,1,0:T(8,128)} %number.3, s32[2,64]{1,0:T(2,128)S(1)} %copy-done.4, f32[3,256]{1,0:T(4,128)S(1)} %copy-done.2, ...), custom_call_target="tpu_custom_call" | custom-call | flops 1000000 | bytes 1000000 | tf_op jit(solution)/shard_map/local/pallas_call | solution.py:366
  15.6 0.7 %collective-permute-start = (f32[16,80,128]{2,1,0:T(8,128)S(1)}, f32[16,80,128]{2,1,0:T(8,128)S(1)}, u32[]{:S(2)}, u32[]{:S(2)}) collective-permute-start(f32[16,80,128]{2,1,0:T(8,128)S(1)} %get-tuple-element.12), channel_id=1, source_target_pairs={{0,8},{1,9},{2,10},{3,11},{4,12},{5,13},{6,14},{7,15},{8,0},{9,1},... | collective-permute-start | bytes 1966088 | tf_op jit(solution)/shard_map/ppermute | solution.py:387
  16.3 0.1 collective-permute-start.1
  16.4 1.6 %collective-permute-done.refs_0_ = f32[16,80,128]{2,1,0:T(8,128)S(1)} collective-permute-done((f32[16,80,128]{2,1,0:T(8,128)S(1)}, f32[16,80,128]{2,1,0:T(8,128)S(1)}, u32[]{:S(2)}, u32[]{:S(2)}) %collective-permute-start) | collective-permute-done | bytes 655392 | tf_op jit(solution)/shard_map/ppermute | solution.py:387
  18.0 0.9 %collective-permute-done.1.refs_1_ = f32[16,80,128]{2,1,0:T(8,128)S(1)} collective-permute-done((f32[16,80,128]{2,1,0:T(8,128)S(1)}, f32[16,80,128]{2,1,0:T(8,128)S(1)}, u32[]{:S(2)}, u32[]{:S(2)}) %collective-permute-start.1) | collective-permute-done | bytes 655392 | tf_op jit(solution)/shard_map/ppermute | solution.py:387
  19.0 1.1 %near.1.base = f32[64,80,256]{2,1,0:T(8,128)S(1)} custom-call(f32[64,80,256]{2,1,0:T(8,128)S(1)} %get-tuple-element.10.base, bf16[2,2,256,256]{3,2,1,0:T(8,128)(2,1)S(1)} %get-tuple-element.11.came, f32[16,80,128]{2,1,0:T(8,128)S(1)} %collective-permute-done.refs_0_, f32[16,80,128]{2,1,0:T(8,128)S(1)} %collective-permute-done.1.refs_1_), custom_call_target="tpu_custom_call", output_to_operand_aliasing={{}: (0, {})} | custom-call | flops 1000000 | bytes 1000000 | tf_op jit(solution)/shard_map/near/pallas_call | solution.py:389
  20.1 6.4 %collective-permute-done.2.far = f32[16,152,128]{2,1,0:T(8,128)S(1)} collective-permute-done((f32[16,152,128]{2,1,0:T(8,128)}, f32[16,152,128]{2,1,0:T(8,128)S(1)}, u32[]{:S(2)}, u32[]{:S(2)}) %collective-permute-start.2) | collective-permute-done | bytes 1245216 | tf_op jit(solution)/shard_map/ppermute | solution.py:363
  26.6 2.7 %update.1 = f32[64,16,256]{2,1,0:T(8,128)} custom-call(f32[64,80,256]{2,1,0:T(8,128)S(1)} %near.1.base, bf16[2,2,256,256]{3,2,1,0:T(8,128)(2,1)S(1)} %get-tuple-element.11.came, bf16[48,96]{1,0:T(8,128)(2,1)S(1)} %get-tuple-element.14.band, f32[16,152,128]{2,1,0:T(8,128)S(1)} %collective-permute-done.2.far), custom_call_target="tpu_custom_call" | custom-call | flops 1000000 | bytes 1000000 | tf_op jit(solution)/shard_map/update/pallas_call | solution.py:400
Async XLA Ops:
  0.0 8.0 %copy-start = (f32[5,128,128]{2,1,0:T(8,128)S(1)}, f32[5,128,128]{2,1,0:T(8,128)}, u32[]{:S(2)}) copy-start(f32[5,128,128]{2,1,0:T(8,128)} %constant.2.clone.refs_7_.refs_5_) | copy-start | bytes 983044
  0.0 8.1 %copy-start.6 = (f32[128]{0:T(128)S(1)}, f32[128]{0:T(128)}, u32[]{:S(2)}) copy-start(f32[128]{0:T(128)} %param.14) | copy-start | bytes 1540
  0.0 8.1 %copy-start.7 = (f32[128]{0:T(128)S(1)}, f32[128]{0:T(128)}, u32[]{:S(2)}) copy-start(f32[128]{0:T(128)} %param.15) | copy-start | bytes 1540
  0.0 8.1 %copy-start.4 = (s32[2,64]{1,0:T(2,128)S(1)}, s32[2,64]{1,0:T(2,128)}, u32[]{:S(2)}) copy-start(s32[2,64]{1,0:T(2,128)} %refs_0_.3) | copy-start | bytes 1540
  0.0 8.1 %copy-start.1 = (f32[128,128]{1,0:T(8,128)S(1)}, f32[128,128]{1,0:T(8,128)}, u32[]{:S(2)}) copy-start(f32[128,128]{1,0:T(8,128)} %refs_1_.3) | copy-start | bytes 196612
  0.0 8.1 %copy-start.5 = (s32[2,128]{1,0:T(2,128)S(1)}, s32[2,128]{1,0:T(2,128)}, u32[]{:S(2)}) copy-start(s32[2,128]{1,0:T(2,128)} %refs_4_.1) | copy-start | bytes 3076
  0.0 8.1 %copy-start.2 = (f32[3,256]{1,0:T(4,128)S(1)}, f32[3,256]{1,0:T(4,128)}, u32[]{:S(2)}) copy-start(f32[3,256]{1,0:T(4,128)} %refs_1_.2) | copy-start | bytes 9220
  0.0 8.1 %copy-start.3 = (s32[3,256]{1,0:T(4,128)S(1)}, s32[3,256]{1,0:T(4,128)}, u32[]{:S(2)}) copy-start(s32[3,256]{1,0:T(4,128)} %refs_2_.1) | copy-start | bytes 9220
  6.0 20.5 %collective-permute-start.2 = (f32[16,152,128]{2,1,0:T(8,128)}, f32[16,152,128]{2,1,0:T(8,128)S(1)}, u32[]{:S(2)}, u32[]{:S(2)}) collective-permute-start(f32[16,152,128]{2,1,0:T(8,128)} %halo0.1), channel_id=1, source_target_pairs={{8,16},{9,17},{10,18},{11,19},{12,20},{13,21},{14,22},{15,23},{16,... | collective-permute-start | bytes 3735560 | tf_op jit(solution)/shard_map/ppermute | solution.py:363
  15.6 2.4 %collective-permute-start = (f32[16,80,128]{2,1,0:T(8,128)S(1)}, f32[16,80,128]{2,1,0:T(8,128)S(1)}, u32[]{:S(2)}, u32[]{:S(2)}) collective-permute-start(f32[16,80,128]{2,1,0:T(8,128)S(1)} %get-tuple-element.12), channel_id=1, source_target_pairs={{0,8},{1,9},{2,10},{3,11},{4,12},{5,13},{6,14},{7,15},{8,0},{9,1},... | collective-permute-start | bytes 1966088 | tf_op jit(solution)/shard_map/ppermute | solution.py:387
  16.3 2.7 %collective-permute-start.1 = (f32[16,80,128]{2,1,0:T(8,128)S(1)}, f32[16,80,128]{2,1,0:T(8,128)S(1)}, u32[]{:S(2)}, u32[]{:S(2)}) collective-permute-start(f32[16,80,128]{2,1,0:T(8,128)S(1)} %get-tuple-element.13), channel_id=1, source_target_pairs={{0,8},{1,9},{2,10},{3,11},{4,12},{5,13},{6,14},{7,15},{8,0},{9,1},... | collective-permute-start | bytes 1966088 | tf_op jit(solution)/shard_map/ppermute | solution.py:387
